TPU v7x, 512 devices: a whole 4x4x16 slice. The times are simulated.
512 devices in a mesh: gx: 8 (over z_hi, y), gy: 8 (over x, core), gz: 8 (over z_lo).
Axes of the slice: x: 4, y: 4, z: 16 (z_hi: 2, z_lo: 8; z = z_hi * 8 + z_lo), core: 2. Of those that a mesh axis runs over, the one named last changes fastest.
Arguments:
- tokens: bfloat16 [2048, 6144], P('gy', ('gz', 'gx')), may hold values from -6 to 6
- up_weight: bfloat16 [6144, 24576], P(('gz', 'gy'), 'gx'), may hold values from -0.078125 to 0.078125
- down_weight: bfloat16 [24576, 6144], P('gx', ('gz', 'gy')), may hold values from -0.0390625 to 0.0390625
- grad_output: bfloat16 [2048, 6144], P('gy', ('gz', 'gx')), may hold values from -6 to 6
Outputs:
- output: bfloat16 [2048, 6144], P('gy', ('gz', 'gx'))
- grad_tokens: bfloat16 [2048, 6144], P('gy', ('gz', 'gx'))
All inputs are finite; a program needn't handle non-finite values.
Results may differ from a plain program's by a relative error of at most 0.027.
Values may be sent and summed in bfloat16 or wider, within the bound.
No kernel may reach another device: no remote copies, remote signals or barrier semaphores. Data moves between devices by JAX's collectives and lax.ppermute only.
A program may use at most 64 MiB of HBM per device.

v0:
```python
import math

import jax
import jax.numpy as jnp
from jax import lax
from jax.sharding import PartitionSpec as P

root_scale = math.sqrt(2.0 / math.pi)
cubic_term = 0.044715


def gelu_value(hidden):
    curved = jnp.tanh(root_scale * (hidden + cubic_term * hidden * hidden * hidden))
    return 0.5 * hidden * (1.0 + curved)


def gelu_slope(hidden):
    curved = jnp.tanh(root_scale * (hidden + cubic_term * hidden * hidden * hidden))
    return 0.5 * (1.0 + curved) + 0.5 * hidden * (1.0 - curved * curved) * root_scale * (
        1.0 + 3.0 * cubic_term * hidden * hidden
    )


def combine_rows(partial_value):
    return lax.psum(partial_value.astype(jnp.bfloat16), "gz").astype(jnp.float32)


def finish_sums(partial_value):
    return lax.psum_scatter(
        partial_value.astype(jnp.bfloat16), "gx", scatter_dimension=1, tiled=True
    )


def against(left_side, right_side):
    return lax.dot_general(
        left_side, right_side, (((1,), (1,)), ((), ())), preferred_element_type=jnp.float32
    )


def local(tokens, up_weight, down_weight, grad_output):
    rows_in, grads_in = (
        lax.all_gather(tokens, "gx", axis=1, tiled=True),
        lax.all_gather(grad_output, "gx", axis=1, tiled=True),
    )
    up_block, down_block = (
        lax.all_gather(up_weight, "gy", axis=0, tiled=True),
        lax.all_gather(down_weight, "gy", axis=1, tiled=True),
    )
    hidden = combine_rows(jnp.dot(rows_in, up_block, preferred_element_type=jnp.float32))
    activated = gelu_value(hidden).astype(jnp.bfloat16)
    output = finish_sums(jnp.dot(activated, down_block, preferred_element_type=jnp.float32))
    grad_act = combine_rows(against(grads_in, down_block))
    grad_hidden = (grad_act * gelu_slope(hidden)).astype(jnp.bfloat16)
    grad_tokens = finish_sums(against(grad_hidden, up_block))
    return (output, grad_tokens)


def solution(mesh):
    in_specs = (
        P("gy", ("gz", "gx")),
        P(("gz", "gy"), "gx"),
        P("gx", ("gz", "gy")),
        P("gy", ("gz", "gx")),
    )
    out_specs = (P("gy", ("gz", "gx")), P("gy", ("gz", "gx")))
    return jax.shard_map(local, mesh=mesh, in_specs=in_specs, out_specs=out_specs, check_vma=False)
```

profile of v0, /device:TPU:24, one launch (start us, length us, event | category | flops | bytes accessed | tf_op | source)
XLA Modules:
  0.0 543.2 jit_solution(7581180157762038772)
XLA Ops:
  7.2 0.0 all-gather.5.cloned.1.call-start
  7.2 0.7 all-gather.5.cloned.1.call-update
  7.9 0.0 all-gather.3.cloned.1.call-start
  7.9 0.7 all-gather.3.cloned.1.call-update
  8.6 0.0 all-reduce.3.cloned.1.call-start
  8.7 65.9 %all_gather.12 = bf16[256,768]{0,1:T(8,128)(2,1)S(1)} all-gather(bf16[256,96]{0,1:T(8,128)(2,1)} %param.4), channel_id=1, replica_groups=mesh['gx'=8,'gy'=8,'gz'=8] {'gx'}, dimensions={1}, use_global_device_ids=true | all-gather | bytes 442368 | tf_op jit(solution)/shard_map/all_gather | solution.py:42
  74.6 63.9 %all_gather.15 = bf16[256,768]{0,1:T(8,128)(2,1)S(1)} all-gather(bf16[256,96]{0,1:T(8,128)(2,1)} %param.7), channel_id=1, replica_groups=mesh['gx'=8,'gy'=8,'gz'=8] {'gx'}, dimensions={1}, use_global_device_ids=true | all-gather | bytes 442368 | tf_op jit(solution)/shard_map/all_gather | solution.py:43
  138.5 0.0 all-gather.5.cloned.1.call-done
  138.5 4.9 convolution_convert_fusion
  143.4 0.0 all-gather.3.cloned.1.call-done
  143.4 4.9 convolution_convert_fusion.1
  148.3 0.0 all-reduce.3.cloned.1.call-update
  148.3 0.0 reduce-scatter.5.cloned.1.call-start
  148.3 168.9 %all-reduce.3.cloned.1.call-done = (bf16[256,3072]{1,0:T(8,128)(2,1)}, bf16[256,3072]{1,0:T(8,128)(2,1)}) async-done(((bf16[256,3072]{1,0:T(8,128)(2,1)}, bf16[256,3072]{1,0:T(8,128)(2,1)}), (bf16[256,3072]{1,0:T(8,128)(2,1)}, bf16[256,3072]{1,0:T(8,128)(2,1)})) %all-reduce.3.cloned.1.call-update) | async-done | bytes 3145744 | tf_op jit(solution)/shard_map/psum | solution.py:25
  317.2 0.0 copy-start
  317.2 7.4 %fusion.22 = bf16[256,768]{0,1:T(8,128)(2,1)} fusion(bf16[768,3072]{1,0:T(8,128)(2,1)} %all-gather.3.cloned.1.call-done, bf16[256,3072]{1,0:T(8,128)(2,1)} %get-tuple-element.2, bf16[256,3072]{1,0:T(8,128)(2,1)} %get-tuple-element.3), kind=kOutput, calls=%fused_computation.27 | convolution fusion | flops 1224671232 | bytes 8257536 | tf_op jit(solution)/shard_map/dot_general | solution.py:35
  324.7 0.0 reduce-scatter.5.cloned.1.call-update
  324.7 0.0 reduce-scatter.3.cloned.1.call-start
  324.7 0.0 copy-done
  324.7 4.6 fusion.19
  329.4 0.0 reduce-scatter.3.cloned.1.call-update
  329.4 100.7 %reduce-scatter.5.cloned.1.call-done = bf16[256,96]{0,1:T(8,128)(2,1)} async-done(((bf16[256,768]{0,1:T(8,128)(2,1)}), bf16[256,96]{0,1:T(8,128)(2,1)}) %reduce-scatter.5.cloned.1.call-update) | async-done | bytes 49168 | tf_op jit(solution)/shard_map/reduce_scatter | solution.py:29
  430.1 106.6 %reduce-scatter.3.cloned.1.call-done = bf16[256,96]{0,1:T(8,128)(2,1)} async-done(((bf16[256,768]{0,1:T(8,128)(2,1)}), bf16[256,96]{0,1:T(8,128)(2,1)}) %reduce-scatter.3.cloned.1.call-update) | async-done | bytes 49168 | tf_op jit(solution)/shard_map/reduce_scatter | solution.py:29
Async XLA Ops:
  7.2 131.3 %all-gather.5.cloned.1.call-start = ((), (), s32[]{:S(2)}) async-start(), calls=%async_computation.3 | async-start | bytes 5308416 | tf_op jit(solution)/shard_map/all_gather | solution.py:47
  7.9 135.5 %all-gather.3.cloned.1.call-start = ((), (), s32[]{:S(2)}) async-start(), calls=%async_computation.2 | async-start | bytes 5308416 | tf_op jit(solution)/shard_map/all_gather | solution.py:46
  8.6 308.6 %all-reduce.3.cloned.1.call-start = ((), (), s32[]{:S(2)}) async-start(), calls=%async_computation.6 | async-start | bytes 6291456 | tf_op jit(solution)/shard_map/psum | solution.py:25
  148.3 281.8 %reduce-scatter.5.cloned.1.call-start = ((), (), s32[]{:S(2)}) async-start(), calls=%async_computation.5 | async-start | bytes 442368 | tf_op jit(solution)/shard_map/reduce_scatter | solution.py:29
  317.2 7.5 %copy-start = (bf16[256,3072]{1,0:T(8,128)(2,1)S(1)}, bf16[256,3072]{1,0:T(8,128)(2,1)}, u32[]{:S(2)}) copy-start(bf16[256,3072]{1,0:T(8,128)(2,1)} %get-tuple-element.2) | copy-start | bytes 4718596
  324.7 212.0 %reduce-scatter.3.cloned.1.call-start = ((), (), s32[]{:S(2)}) async-start(), calls=%async_computation.4 | async-start | bytes 442368 | tf_op jit(solution)/shard_map/reduce_scatter | solution.py:29
Sparse Core Ops, SparseCore 0:
  10.1 46.1 all-gather.4
  58.4 42.0 all-gather.2
  148.4 168.7 all-reduce.2
  324.8 105.2 reduce-scatter.4
  435.0 101.6 reduce-scatter.2
where the time goes:
time: 544 us; the launch traced here: 543 us
  waiting for transfers between devices  378 us (69%)
  blocking collectives  130 us (24%)
  matrix products  21.9 us (4%)
  between operations  13.8 us (3%)
    reduce_scatter x2, waiting for transfers between devices, finish_sums(): lax.psum_scatter(partial_value.astype(jnp.bfloat16), 'gx', scatter_dimens...  207 us
    psum x1, waiting for transfers between devices, combine_rows(): lax.psum(partial_value.astype(jnp.bfloat16), 'gz').astype(jnp.float32)  169 us
    all_gather x1, blocking collectives, local(): lax.all_gather(tokens, 'gx', axis=1, tiled=True)  65.9 us
    all_gather x1, blocking collectives, local(): lax.all_gather(grad_output, 'gx', axis=1, tiled=True)  63.9 us
    dot_general x2, matrix products, against(): lax.dot_general(left_side, right_side, (((1,), (1,)), ((), ())), preferre...  12.3 us
  transfers between devices with their start and end apart: 5, of which 3 were waited for; matrix products, arithmetic and copies ran while one was open for 2% of the time, Pallas kernels for 0%

commit v1 on v0

v1 whole, which is shorter than its diff:
```python
import math

import jax
import jax.numpy as jnp
from jax import lax
from jax.sharding import Mesh
from jax.sharding import PartitionSpec as P

root_scale = math.sqrt(2.0 / math.pi)
cubic_term = 0.044715
SWAP = [(0, 1), (1, 0)]
AXES = ("zh", "y", "x", "core", "z4", "z2", "z1")


def gelu_value(hidden):
    curved = jnp.tanh(root_scale * (hidden + cubic_term * hidden * hidden * hidden))
    return 0.5 * hidden * (1.0 + curved)


def gelu_slope(hidden):
    curved = jnp.tanh(root_scale * (hidden + cubic_term * hidden * hidden * hidden))
    return 0.5 * (1.0 + curved) + 0.5 * hidden * (1.0 - curved * curved) * root_scale * (
        1.0 + 3.0 * cubic_term * hidden * hidden
    )


def swap(array, axis):
    return lax.ppermute(array, axis, SWAP)


def swap_blocks(array, bit, axis):
    return jnp.where(bit == 1, jnp.flip(array, axis), array)


def own_order(columns):
    rows = columns.shape[0]
    blocks = columns.reshape(rows, 2, 2, 2, 32)
    for axis, name in ((1, "z1"), (2, "z2"), (3, "z4")):
        blocks = swap_blocks(blocks, lax.axis_index(name), axis)
    return blocks.reshape(rows, 256)


def scatter_sum(partial_value):
    total = partial_value
    for name in ("z1", "z2", "z4"):
        half = total.shape[0] // 2
        sent = total[half:].astype(jnp.bfloat16)
        total = total[:half].astype(jnp.bfloat16).astype(jnp.float32) + swap(sent, name).astype(jnp.float32)
    return total


def gather_tokens(rows):
    for name in ("z4", "z2", "z1"):
        rows = jnp.concatenate([rows, swap(rows, name)], 0)
    return rows


def rows_of(shards):
    both = jnp.stack([shards, swap(shards, "zh")])
    all_y = lax.all_gather(both.reshape(384, 256), "y", axis=0, tiled=True)
    all_y = all_y.reshape(4, 2, 2, 96, 256).transpose(2, 1, 0, 3, 4)
    all_y = swap_blocks(all_y, lax.axis_index("zh"), 1).reshape(2, 768, 256)
    return all_y[0], all_y[1]


def finish(partial_value):
    blocks = partial_value.astype(jnp.bfloat16).reshape(2, 4, 96, 256)
    blocks = swap_blocks(blocks, lax.axis_index("zh"), 0).transpose(1, 0, 2, 3)
    parts = lax.all_to_all(blocks, "y", 0, 0, tiled=True)
    total = parts.astype(jnp.float32).sum(0)
    other = swap(total[1].astype(jnp.bfloat16), "zh")
    return (total[0] + other.astype(jnp.float32)).astype(jnp.bfloat16)


def contract(left, right, dims):
    return lax.dot_general(left, right, (dims, ((), ())), preferred_element_type=jnp.float32)


def local(tokens, up_weight, down_weight, grad_output):
    shards = own_order(jnp.concatenate([tokens.T, grad_output.T], 0))
    up_block = lax.all_gather(up_weight, ("x", "core"), axis=0, tiled=True)
    down_block = lax.all_gather(down_weight.T, ("x", "core"), axis=0, tiled=True)
    rows_in, grads_in = rows_of(shards)
    hidden = scatter_sum(contract(rows_in, up_block, ((0,), (0,))))
    activated = gather_tokens(gelu_value(hidden).astype(jnp.bfloat16))
    output = finish(contract(down_block, activated, ((1,), (1,))))
    grad_act = scatter_sum(contract(grads_in, down_block, ((0,), (0,))))
    grad_hidden = gather_tokens((grad_act * gelu_slope(hidden)).astype(jnp.bfloat16))
    grad_tokens = finish(contract(up_block, grad_hidden, ((1,), (1,))))
    return (own_order(output).T, own_order(grad_tokens).T)


def solution(mesh):
    fine = Mesh(mesh.devices.reshape(2, 4, 4, 2, 2, 2, 2), AXES)
    gx, gy, gz = ("zh", "y"), ("x", "core"), ("z4", "z2", "z1")
    in_specs = (P(gy, gz + gx), P(gz + gy, gx), P(gx, gz + gy), P(gy, gz + gx))
    out_specs = (P(gy, gz + gx), P(gy, gz + gx))
    return jax.shard_map(local, mesh=fine, in_specs=in_specs, out_specs=out_specs, check_vma=False)
```

time: 544 us -> 325 us (0.60)
  waiting for transfers between devices: 378 us -> 189 us
  blocking collectives: 130 us -> 14.1 us
  starting transfers between devices: 0.2 us -> 84.7 us
  matrix products: 21.9 us -> 12.7 us
  local copies, waits for them, and re-layouts: 0.01 us -> 5.84 us
    reduce_scatter x2 -> x0, waiting for transfers between devices: 207 us -> none  [finish_sums(): lax.psum_scatter(partial_value.astype(jnp.bfloat16), 'gx', scatter_dimens...]
    psum x1 -> x0, waiting for transfers between devices: 169 us -> none  [combine_rows(): lax.psum(partial_value.astype(jnp.bfloat16), 'gz').astype(jnp.float32)]
    ppermute x0 -> x15, waiting for transfers between devices: none -> 140 us  [swap(): return lax.ppermute(array, axis, SWAP)]
    all_gather x2 -> x1, blocking collectives: 130 us -> 14.1 us  [rows_of(): all_y = lax.all_gather(both.reshape(384, 256), 'y', axis=0, tiled=True)]
    ppermute x0 -> x15, starting transfers between devices: none -> 75.1 us  [swap(): return lax.ppermute(array, axis, SWAP)]
    all_gather x2, waiting for transfers between devices: 0.01 us -> 48.5 us  [the longest x1 36.9 us: local(): lax.all_gather(down_weight.T, ('x', 'core'), axis=0, tiled=True)]
    all_to_all x0 -> x2, starting transfers between devices: none -> 9.55 us  [finish(): parts = lax.all_to_all(blocks, 'y', 0, 0, tiled=True)]
    dot_general x4, matrix products: 21.9 us -> 12.7 us  [contract(): lax.dot_general(left, right, (dims, ((), ())), preferred_element_type=jnp...]
  transfers between devices with their start and end apart: 5 -> 19, of which waited for: 3 -> 11; matrix products, arithmetic and copies ran while one was open for 2% -> 6% of each run, Pallas kernels for 0% -> 0%
where the time goes in v1:
time: 325 us
  waiting for transfers between devices  189 us (58%)
  starting transfers between devices  84.7 us (26%)
  between operations  14.6 us (4%)
  blocking collectives  14.1 us (4%)
  matrix products  12.7 us (4%)
  local copies, waits for them, and re-layouts  5.84 us (2%)
    ppermute x15, waiting for transfers between devices, swap(): return lax.ppermute(array, axis, SWAP)  140 us
    ppermute x15, starting transfers between devices, swap(): return lax.ppermute(array, axis, SWAP)  75.1 us
    all_gather x1, waiting for transfers between devices, local(): lax.all_gather(down_weight.T, ('x', 'core'), axis=0, tiled=True)  36.9 us
    all_gather x1, blocking collectives, rows_of(): all_y = lax.all_gather(both.reshape(384, 256), 'y', axis=0, tiled=True)  14.1 us
    dot_general x4, matrix products, contract(): lax.dot_general(left, right, (dims, ((), ())), preferred_element_type=jnp...  12.7 us
    all_gather x1, waiting for transfers between devices, local(): up_block = lax.all_gather(up_weight, ('x', 'core'), axis=0, tiled=True)  11.6 us
    all_to_all x2, starting transfers between devices, finish(): parts = lax.all_to_all(blocks, 'y', 0, 0, tiled=True)  9.55 us
  transfers between devices with their start and end apart: 19, of which 11 were waited for; matrix products, arithmetic and copies ran while one was open for 6% of the time, Pallas kernels for 0%

profile of v1, /device:TPU:24, one launch (start us, length us, event | category | flops | bytes accessed | tf_op | source)
XLA Modules:
  0.0 324.5 jit_solution(1100044821605179423)
XLA Ops:
  10.7 15.7 %collective-permute-start = (bf16[192,256]{0,1:T(8,128)(2,1)S(1)}, bf16[192,256]{0,1:T(8,128)(2,1)S(1)}, u32[]{:S(2)}, u32[]{:S(2)}) collective-permute-start(bf16[192,256]{0,1:T(8,128)(2,1)S(1)} %bitcast.63), channel_id=1, source_target_pairs={{0,256},{256,0},{1,257},{257,1},{2,258},{258,2},{3,259},{259,3},{4... | collective-permute-start | bytes 294920 | tf_op jit(solution)/shard_map/ppermute | solution.py:28
  26.4 3.8 %collective-permute-done = bf16[192,256]{0,1:T(8,128)(2,1)S(1)} collective-permute-done((bf16[192,256]{0,1:T(8,128)(2,1)S(1)}, bf16[192,256]{0,1:T(8,128)(2,1)S(1)}, u32[]{:S(2)}, u32[]{:S(2)}) %collective-permute-start) | collective-permute-done | bytes 98336 | tf_op jit(solution)/shard_map/ppermute | solution.py:28
  30.4 14.1 %all_gather.9 = bf16[1536,256]{1,0:T(8,128)(2,1)S(1)} all-gather(bf16[384,256]{1,0:T(8,128)(2,1)S(1)} %bitcast.60), channel_id=1, replica_groups=mesh['zh'=2,'y'=4,'x'=4,'core'=2,'z4'=2,'z2'=2,'z1'=2] {'y'}, dimensions={0}, use_global_device_ids=true | all-gather | bytes 983040 | tf_op jit(solution)/shard_map/all_gather | solution.py:60
  44.7 11.6 %all-gather.3.cloned.1.call-done = bf16[768,3072]{1,0:T(8,128)(2,1)} async-done(((bf16[96,3072]{1,0:T(8,128)(2,1)}), bf16[768,3072]{1,0:T(8,128)(2,1)}) %all-gather.3.cloned.1.call-update) | async-done | bytes 4718608 | tf_op jit(solution)/shard_map/all_gather | solution.py:81
  56.3 3.7 %convolution_convert_fusion.1 = bf16[256,3072]{1,0:T(8,128)(2,1)S(1)} fusion(bf16[768,256]{1,0:T(8,128)(2,1)S(1)} %bitcast.56, bf16[768,3072]{1,0:T(8,128)(2,1)} %all-gather.3.cloned.1.call-done), kind=kOutput, calls=%fused_computation.1 | convolution fusion | flops 1208745984 | bytes 6684672 | tf_op jit(solution)/shard_map/dot_general | solution.py:76
  60.1 3.5 %collective-permute-start.1 = (bf16[128,3072]{1,0:T(8,128)(2,1)S(1)}, bf16[128,3072]{1,0:T(8,128)(2,1)}, u32[]{:S(2)}, u32[]{:S(2)}) collective-permute-start(bf16[128,3072]{1,0:T(8,128)(2,1)S(1)} %slice.90), channel_id=1, source_target_pairs={{0,1},{1,0},{2,3},{3,2},{4,5},{5,4},{6,7},{7,6},{8,9},{9,8},{10,11... | collective-permute-start | bytes 2359304 | tf_op jit(solution)/shard_map/ppermute | solution.py:28
  63.6 36.9 %all-gather.5.cloned.1.call-done = bf16[768,3072]{1,0:T(8,128)(2,1)} async-done(((bf16[96,3072]{1,0:T(8,128)(2,1)}), bf16[768,3072]{1,0:T(8,128)(2,1)}) %all-gather.5.cloned.1.call-update) | async-done | bytes 4718608 | tf_op jit(solution)/shard_map/all_gather | solution.py:82
  100.5 3.7 %convolution_convert_fusion = bf16[256,3072]{1,0:T(8,128)(2,1)S(1)} fusion(bf16[768,256]{1,0:T(8,128)(2,1)S(1)} %bitcast.57, bf16[768,3072]{1,0:T(8,128)(2,1)} %all-gather.5.cloned.1.call-done), kind=kOutput, calls=%fused_computation | convolution fusion | flops 1208745984 | bytes 6684672 | tf_op jit(solution)/shard_map/dot_general | solution.py:76
  104.3 3.5 %collective-permute-start.8 = (bf16[128,3072]{1,0:T(8,128)(2,1)S(1)}, bf16[128,3072]{1,0:T(8,128)(2,1)S(1)}, u32[]{:S(2)}, u32[]{:S(2)}) collective-permute-start(bf16[128,3072]{1,0:T(8,128)(2,1)S(1)} %slice.99), channel_id=1, source_target_pairs={{0,1},{1,0},{2,3},{3,2},{4,5},{5,4},{6,7},{7,6},{8,9},{9,8},{10,11... | collective-permute-start | bytes 2359304 | tf_op jit(solution)/shard_map/ppermute | solution.py:28
  109.3 4.5 %collective-permute-start.2 = (bf16[64,3072]{1,0:T(8,128)(2,1)S(1)}, bf16[64,3072]{1,0:T(8,128)(2,1)S(1)}, u32[]{:S(2)}, u32[]{:S(2)}) collective-permute-start(bf16[64,3072]{1,0:T(8,128)(2,1)S(1)} %slice.92), channel_id=1, source_target_pairs={{0,2},{2,0},{1,3},{3,1},{4,6},{6,4},{5,7},{7,5},{8,10},{10,8},{9,1... | collective-permute-start | bytes 1179656 | tf_op jit(solution)/shard_map/ppermute | solution.py:28
  113.8 20.6 %collective-permute-done.8 = bf16[128,3072]{1,0:T(8,128)(2,1)S(1)} collective-permute-done((bf16[128,3072]{1,0:T(8,128)(2,1)S(1)}, bf16[128,3072]{1,0:T(8,128)(2,1)S(1)}, u32[]{:S(2)}, u32[]{:S(2)}) %collective-permute-start.8) | collective-permute-done | bytes 786464 | tf_op jit(solution)/shard_map/ppermute | solution.py:28
  134.6 3.5 %collective-permute-start.9 = (bf16[64,3072]{1,0:T(8,128)(2,1)S(1)}, bf16[64,3072]{1,0:T(8,128)(2,1)S(1)}, u32[]{:S(2)}, u32[]{:S(2)}) collective-permute-start(bf16[64,3072]{1,0:T(8,128)(2,1)S(1)} %slice.101), channel_id=1, source_target_pairs={{0,2},{2,0},{1,3},{3,1},{4,6},{6,4},{5,7},{7,5},{8,10},{10,8},{9,1... | collective-permute-start | bytes 1179656 | tf_op jit(solution)/shard_map/ppermute | solution.py:28
  138.2 7.8 %collective-permute-start.3 = (bf16[32,3072]{1,0:T(8,128)(2,1)S(1)}, bf16[32,3072]{1,0:T(8,128)(2,1)S(1)}, u32[]{:S(2)}, u32[]{:S(2)}) collective-permute-start(bf16[32,3072]{1,0:T(8,128)(2,1)S(1)} %slice.94), channel_id=1, source_target_pairs={{0,4},{4,0},{1,5},{5,1},{2,6},{6,2},{3,7},{7,3},{8,12},{12,8},{9,1... | collective-permute-start | bytes 589832 | tf_op jit(solution)/shard_map/ppermute | solution.py:28
  146.0 18.6 %collective-permute-done.9 = bf16[64,3072]{1,0:T(8,128)(2,1)S(1)} collective-permute-done((bf16[64,3072]{1,0:T(8,128)(2,1)S(1)}, bf16[64,3072]{1,0:T(8,128)(2,1)S(1)}, u32[]{:S(2)}, u32[]{:S(2)}) %collective-permute-start.9) | collective-permute-done | bytes 393248 | tf_op jit(solution)/shard_map/ppermute | solution.py:28
  164.8 4.5 %collective-permute-start.10 = (bf16[32,3072]{1,0:T(8,128)(2,1)S(1)}, bf16[32,3072]{1,0:T(8,128)(2,1)S(1)}, u32[]{:S(2)}, u32[]{:S(2)}) collective-permute-start(bf16[32,3072]{1,0:T(8,128)(2,1)S(1)} %slice.103), channel_id=1, source_target_pairs={{0,4},{4,0},{1,5},{5,1},{2,6},{6,2},{3,7},{7,3},{8,12},{12,8},{9,1... | collective-permute-start | bytes 589832 | tf_op jit(solution)/shard_map/ppermute | solution.py:28
  169.3 19.8 %collective-permute-done.10 = bf16[32,3072]{1,0:T(8,128)(2,1)S(1)} collective-permute-done((bf16[32,3072]{1,0:T(8,128)(2,1)S(1)}, bf16[32,3072]{1,0:T(8,128)(2,1)S(1)}, u32[]{:S(2)}, u32[]{:S(2)}) %collective-permute-start.10) | collective-permute-done | bytes 196640 | tf_op jit(solution)/shard_map/ppermute | solution.py:28
  189.4 1.9 collective-permute-start.11
  191.4 13.4 %collective-permute-done.11 = bf16[32,3072]{1,0:T(8,128)(2,1)S(1)} collective-permute-done((bf16[32,3072]{1,0:T(8,128)(2,1)S(1)}, bf16[32,3072]{1,0:T(8,128)(2,1)S(1)}, u32[]{:S(2)}, u32[]{:S(2)}) %collective-permute-start.11) | collective-permute-done | bytes 196640 | tf_op jit(solution)/shard_map/ppermute | solution.py:28
  204.8 1.9 collective-permute-start.12
  206.7 1.9 collective-permute-start.4
  208.6 22.1 %collective-permute-done.12 = bf16[64,3072]{1,0:T(8,128)(2,1)S(1)} collective-permute-done((bf16[64,3072]{1,0:T(8,128)(2,1)S(1)}, bf16[64,3072]{1,0:T(8,128)(2,1)S(1)}, u32[]{:S(2)}, u32[]{:S(2)}) %collective-permute-start.12) | collective-permute-done | bytes 393248 | tf_op jit(solution)/shard_map/ppermute | solution.py:28
  230.8 1.9 collective-permute-start.13
  232.8 4.2 %collective-permute-start.5 = (bf16[64,3072]{1,0:T(8,128)(2,1)S(1)}, bf16[64,3072]{1,0:T(8,128)(2,1)S(1)}, u32[]{:S(2)}, u32[]{:S(2)}) collective-permute-start(bf16[64,3072]{1,0:T(8,128)(2,1)S(1)} %pad_maximum_fusion.2), channel_id=1, source_target_pairs={{0,2},{2,0},{1,3},{3,1},{4,6},{6,4},{5,7},{7,5},{8,10},{10,8},{9,1... | collective-permute-start | bytes 1179656 | tf_op jit(solution)/shard_map/ppermute | solution.py:28
  237.0 21.4 %collective-permute-done.5 = bf16[64,3072]{1,0:T(8,128)(2,1)S(1)} collective-permute-done((bf16[64,3072]{1,0:T(8,128)(2,1)S(1)}, bf16[64,3072]{1,0:T(8,128)(2,1)S(1)}, u32[]{:S(2)}, u32[]{:S(2)}) %collective-permute-start.5) | collective-permute-done | bytes 393248 | tf_op jit(solution)/shard_map/ppermute | solution.py:28
  258.5 3.8 %collective-permute-start.6 = (bf16[128,3072]{1,0:T(8,128)(2,1)S(1)}, bf16[128,3072]{1,0:T(8,128)(2,1)S(1)}, u32[]{:S(2)}, u32[]{:S(2)}) collective-permute-start(bf16[128,3072]{1,0:T(8,128)(2,1)S(1)} %pad_maximum_fusion), channel_id=1, source_target_pairs={{0,1},{1,0},{2,3},{3,2},{4,5},{5,4},{6,7},{7,6},{8,9},{9,8},{10,11... | collective-permute-start | bytes 2359304 | tf_op jit(solution)/shard_map/ppermute | solution.py:28
  264.8 4.8 %all-to-all-start.1 = ((bf16[4,2,96,256]{3,2,1,0:T(8,128)(2,1)}), bf16[4,2,96,256]{3,2,1,0:T(8,128)(2,1)S(1)}, u32[]{:S(2)}, u32[]{:S(2)}) async-start(bf16[4,2,96,256]{3,2,1,0:T(8,128)(2,1)} %copy.31), calls=%async_computation.1 | async-start | bytes 786432 | tf_op jit(solution)/shard_map/all_to_all | solution.py:69
  269.6 9.7 %collective-permute-done.6 = bf16[128,3072]{1,0:T(8,128)(2,1)S(1)} collective-permute-done((bf16[128,3072]{1,0:T(8,128)(2,1)S(1)}, bf16[128,3072]{1,0:T(8,128)(2,1)S(1)}, u32[]{:S(2)}, u32[]{:S(2)}) %collective-permute-start.6) | collective-permute-done | bytes 786464 | tf_op jit(solution)/shard_map/ppermute | solution.py:28
  279.3 3.8 %fusion.22 = bf16[768,256]{0,1:T(8,128)(2,1)S(1)} fusion(bf16[768,3072]{1,0:T(8,128)(2,1)} %all-gather.5.cloned.1.call-done, bf16[128,3072]{1,0:T(8,128)(2,1)S(1)} %collective-permute-done.6, bf16[64,3072]{1,0:T(8,128)(2,1)S(1)} %collective-permute-done.5, bf16[32,3072]{1,0:T(8,128)(2,1)S(1)} %collective-permute-done.4, ...), kind=kOutput, calls=%fused_computation.22 | convolution fusion | flops 1214447616 | bytes 6684672 | tf_op jit(solution)/shard_map/dot_general | solution.py:76
  284.1 4.8 %all-to-all-start = ((bf16[4,2,96,256]{3,2,1,0:T(8,128)(2,1)}), bf16[4,2,96,256]{3,2,1,0:T(8,128)(2,1)S(1)}, u32[]{:S(2)}, u32[]{:S(2)}) async-start(bf16[4,2,96,256]{3,2,1,0:T(8,128)(2,1)} %copy.26), calls=%async_computation | async-start | bytes 786432 | tf_op jit(solution)/shard_map/all_to_all | solution.py:69
  288.9 11.4 %collective-permute-start.14 = (bf16[96,256]{1,0:T(8,128)(2,1)S(1)}, bf16[96,256]{1,0:T(8,128)(2,1)S(1)}, u32[]{:S(2)}, u32[]{:S(2)}) collective-permute-start(bf16[96,256]{1,0:T(8,128)(2,1)S(1)} %fusion.42), channel_id=1, source_target_pairs={{0,256},{256,0},{1,257},{257,1},{2,258},{258,2},{3,259},{259,3},{4... | collective-permute-start | bytes 147464 | tf_op jit(solution)/shard_map/ppermute | solution.py:28
  300.4 5.2 %collective-permute-start.7 = (bf16[96,256]{1,0:T(8,128)(2,1)S(1)}, bf16[96,256]{1,0:T(8,128)(2,1)S(1)}, u32[]{:S(2)}, u32[]{:S(2)}) collective-permute-start(bf16[96,256]{1,0:T(8,128)(2,1)S(1)} %fusion.41), channel_id=1, source_target_pairs={{0,256},{256,0},{1,257},{257,1},{2,258},{258,2},{3,259},{259,3},{4... | collective-permute-start | bytes 147464 | tf_op jit(solution)/shard_map/ppermute | solution.py:28
  306.6 10.2 %collective-permute-done.7 = bf16[96,256]{1,0:T(8,128)(2,1)S(1)} collective-permute-done((bf16[96,256]{1,0:T(8,128)(2,1)S(1)}, bf16[96,256]{1,0:T(8,128)(2,1)S(1)}, u32[]{:S(2)}, u32[]{:S(2)}) %collective-permute-start.7) | collective-permute-done | bytes 49184 | tf_op jit(solution)/shard_map/ppermute | solution.py:28
  (67 shorter events, 11.9 us)
Async XLA Ops:
  7.2 49.1 %all-gather.3.cloned.1.call-start = ((), (), s32[]{:S(2)}) async-start(), calls=%async_computation.2 | async-start | bytes 5308416 | tf_op jit(solution)/shard_map/all_gather | solution.py:81
  7.9 92.6 %all-gather.5.cloned.1.call-start = ((), (), s32[]{:S(2)}) async-start(), calls=%async_computation.3 | async-start | bytes 5308416 | tf_op jit(solution)/shard_map/all_gather | solution.py:82
  10.7 19.5 %collective-permute-start = (bf16[192,256]{0,1:T(8,128)(2,1)S(1)}, bf16[192,256]{0,1:T(8,128)(2,1)S(1)}, u32[]{:S(2)}, u32[]{:S(2)}) collective-permute-start(bf16[192,256]{0,1:T(8,128)(2,1)S(1)} %bitcast.63), channel_id=1, source_target_pairs={{0,256},{256,0},{1,257},{257,1},{2,258},{258,2},{3,259},{259,3},{4... | collective-permute-start | bytes 294920 | tf_op jit(solution)/shard_map/ppermute | solution.py:28
  60.1 47.7 %collective-permute-start.1 = (bf16[128,3072]{1,0:T(8,128)(2,1)S(1)}, bf16[128,3072]{1,0:T(8,128)(2,1)}, u32[]{:S(2)}, u32[]{:S(2)}) collective-permute-start(bf16[128,3072]{1,0:T(8,128)(2,1)S(1)} %slice.90), channel_id=1, source_target_pairs={{0,1},{1,0},{2,3},{3,2},{4,5},{5,4},{6,7},{7,6},{8,9},{9,8},{10,11... | collective-permute-start | bytes 2359304 | tf_op jit(solution)/shard_map/ppermute | solution.py:28
  104.3 30.0 %collective-permute-start.8 = (bf16[128,3072]{1,0:T(8,128)(2,1)S(1)}, bf16[128,3072]{1,0:T(8,128)(2,1)S(1)}, u32[]{:S(2)}, u32[]{:S(2)}) collective-permute-start(bf16[128,3072]{1,0:T(8,128)(2,1)S(1)} %slice.99), channel_id=1, source_target_pairs={{0,1},{1,0},{2,3},{3,2},{4,5},{5,4},{6,7},{7,6},{8,9},{9,8},{10,11... | collective-permute-start | bytes 2359304 | tf_op jit(solution)/shard_map/ppermute | solution.py:28
  107.8 154.5 %slice-start = ((s8[4718592]{0:T(1024)(128)(4,1)}), s8[4194304]{0:T(1024)(128)(4,1)S(1)}, s32[]{:S(2)}) async-start(s8[4718592]{0:T(1024)(128)(4,1)} %bitcast.53), calls=%async_computation.4 | async-start | bytes 8388608
  109.3 28.8 %collective-permute-start.2 = (bf16[64,3072]{1,0:T(8,128)(2,1)S(1)}, bf16[64,3072]{1,0:T(8,128)(2,1)S(1)}, u32[]{:S(2)}, u32[]{:S(2)}) collective-permute-start(bf16[64,3072]{1,0:T(8,128)(2,1)S(1)} %slice.92), channel_id=1, source_target_pairs={{0,2},{2,0},{1,3},{3,1},{4,6},{6,4},{5,7},{7,5},{8,10},{10,8},{9,1... | collective-permute-start | bytes 1179656 | tf_op jit(solution)/shard_map/ppermute | solution.py:28
  134.6 30.1 %collective-permute-start.9 = (bf16[64,3072]{1,0:T(8,128)(2,1)S(1)}, bf16[64,3072]{1,0:T(8,128)(2,1)S(1)}, u32[]{:S(2)}, u32[]{:S(2)}) collective-permute-start(bf16[64,3072]{1,0:T(8,128)(2,1)S(1)} %slice.101), channel_id=1, source_target_pairs={{0,2},{2,0},{1,3},{3,1},{4,6},{6,4},{5,7},{7,5},{8,10},{10,8},{9,1... | collective-permute-start | bytes 1179656 | tf_op jit(solution)/shard_map/ppermute | solution.py:28
  138.2 124.1 %slice-start.1 = ((s8[4718592]{0:T(1024)(128)(4,1)}), s8[524288]{0:T(1024)(128)(4,1)S(1)}, s32[]{:S(2)}) async-start(s8[4718592]{0:T(1024)(128)(4,1)} %bitcast.53), calls=%async_computation.5 | async-start | bytes 1048576
  138.2 31.1 %collective-permute-start.3 = (bf16[32,3072]{1,0:T(8,128)(2,1)S(1)}, bf16[32,3072]{1,0:T(8,128)(2,1)S(1)}, u32[]{:S(2)}, u32[]{:S(2)}) collective-permute-start(bf16[32,3072]{1,0:T(8,128)(2,1)S(1)} %slice.94), channel_id=1, source_target_pairs={{0,4},{4,0},{1,5},{5,1},{2,6},{6,2},{3,7},{7,3},{8,12},{12,8},{9,1... | collective-permute-start | bytes 589832 | tf_op jit(solution)/shard_map/ppermute | solution.py:28
  164.8 24.3 %collective-permute-start.10 = (bf16[32,3072]{1,0:T(8,128)(2,1)S(1)}, bf16[32,3072]{1,0:T(8,128)(2,1)S(1)}, u32[]{:S(2)}, u32[]{:S(2)}) collective-permute-start(bf16[32,3072]{1,0:T(8,128)(2,1)S(1)} %slice.103), channel_id=1, source_target_pairs={{0,4},{4,0},{1,5},{5,1},{2,6},{6,2},{3,7},{7,3},{8,12},{12,8},{9,1... | collective-permute-start | bytes 589832 | tf_op jit(solution)/shard_map/ppermute | solution.py:28
  189.4 15.3 %collective-permute-start.11 = (bf16[32,3072]{1,0:T(8,128)(2,1)S(1)}, bf16[32,3072]{1,0:T(8,128)(2,1)S(1)}, u32[]{:S(2)}, u32[]{:S(2)}) collective-permute-start(bf16[32,3072]{1,0:T(8,128)(2,1)S(1)} %get-tuple-element.10), channel_id=1, source_target_pairs={{0,4},{4,0},{1,5},{5,1},{2,6},{6,2},{3,7},{7,3},{8,12},{12,8},{9,1... | collective-permute-start | bytes 589832 | tf_op jit(solution)/shard_map/ppermute | solution.py:28
  204.8 26.0 %collective-permute-start.12 = (bf16[64,3072]{1,0:T(8,128)(2,1)S(1)}, bf16[64,3072]{1,0:T(8,128)(2,1)S(1)}, u32[]{:S(2)}, u32[]{:S(2)}) collective-permute-start(bf16[64,3072]{1,0:T(8,128)(2,1)S(1)} %pad_maximum_fusion.3), channel_id=1, source_target_pairs={{0,2},{2,0},{1,3},{3,1},{4,6},{6,4},{5,7},{7,5},{8,10},{10,8},{9,1... | collective-permute-start | bytes 1179656 | tf_op jit(solution)/shard_map/ppermute | solution.py:28
  206.7 26.1 %collective-permute-start.4 = (bf16[32,3072]{1,0:T(8,128)(2,1)S(1)}, bf16[32,3072]{1,0:T(8,128)(2,1)S(1)}, u32[]{:S(2)}, u32[]{:S(2)}) collective-permute-start(bf16[32,3072]{1,0:T(8,128)(2,1)S(1)} %get-tuple-element.11), channel_id=1, source_target_pairs={{0,4},{4,0},{1,5},{5,1},{2,6},{6,2},{3,7},{7,3},{8,12},{12,8},{9,1... | collective-permute-start | bytes 589832 | tf_op jit(solution)/shard_map/ppermute | solution.py:28
  230.8 31.4 %collective-permute-start.13 = (bf16[128,3072]{1,0:T(8,128)(2,1)S(1)}, bf16[128,3072]{1,0:T(8,128)(2,1)S(1)}, u32[]{:S(2)}, u32[]{:S(2)}) collective-permute-start(bf16[128,3072]{1,0:T(8,128)(2,1)S(1)} %pad_maximum_fusion.1), channel_id=1, source_target_pairs={{0,1},{1,0},{2,3},{3,2},{4,5},{5,4},{6,7},{7,6},{8,9},{9,8},{10,11... | collective-permute-start | bytes 2359304 | tf_op jit(solution)/shard_map/ppermute | solution.py:28
  232.8 25.6 %collective-permute-start.5 = (bf16[64,3072]{1,0:T(8,128)(2,1)S(1)}, bf16[64,3072]{1,0:T(8,128)(2,1)S(1)}, u32[]{:S(2)}, u32[]{:S(2)}) collective-permute-start(bf16[64,3072]{1,0:T(8,128)(2,1)S(1)} %pad_maximum_fusion.2), channel_id=1, source_target_pairs={{0,2},{2,0},{1,3},{3,1},{4,6},{6,4},{5,7},{7,5},{8,10},{10,8},{9,1... | collective-permute-start | bytes 1179656 | tf_op jit(solution)/shard_map/ppermute | solution.py:28
  258.5 20.8 %collective-permute-start.6 = (bf16[128,3072]{1,0:T(8,128)(2,1)S(1)}, bf16[128,3072]{1,0:T(8,128)(2,1)S(1)}, u32[]{:S(2)}, u32[]{:S(2)}) collective-permute-start(bf16[128,3072]{1,0:T(8,128)(2,1)S(1)} %pad_maximum_fusion), channel_id=1, source_target_pairs={{0,1},{1,0},{2,3},{3,2},{4,5},{5,4},{6,7},{7,6},{8,9},{9,8},{10,11... | collective-permute-start | bytes 2359304 | tf_op jit(solution)/shard_map/ppermute | solution.py:28
  264.8 19.3 %all-to-all-start.1 = ((bf16[4,2,96,256]{3,2,1,0:T(8,128)(2,1)}), bf16[4,2,96,256]{3,2,1,0:T(8,128)(2,1)S(1)}, u32[]{:S(2)}, u32[]{:S(2)}) async-start(bf16[4,2,96,256]{3,2,1,0:T(8,128)(2,1)} %copy.31), calls=%async_computation.1 | async-start | bytes 786432 | tf_op jit(solution)/shard_map/all_to_all | solution.py:69
  284.1 16.2 %all-to-all-start = ((bf16[4,2,96,256]{3,2,1,0:T(8,128)(2,1)}), bf16[4,2,96,256]{3,2,1,0:T(8,128)(2,1)S(1)}, u32[]{:S(2)}, u32[]{:S(2)}) async-start(bf16[4,2,96,256]{3,2,1,0:T(8,128)(2,1)} %copy.26), calls=%async_computation | async-start | bytes 786432 | tf_op jit(solution)/shard_map/all_to_all | solution.py:69
  288.9 16.7 %collective-permute-start.14 = (bf16[96,256]{1,0:T(8,128)(2,1)S(1)}, bf16[96,256]{1,0:T(8,128)(2,1)S(1)}, u32[]{:S(2)}, u32[]{:S(2)}) collective-permute-start(bf16[96,256]{1,0:T(8,128)(2,1)S(1)} %fusion.42), channel_id=1, source_target_pairs={{0,256},{256,0},{1,257},{257,1},{2,258},{258,2},{3,259},{259,3},{4... | collective-permute-start | bytes 147464 | tf_op jit(solution)/shard_map/ppermute | solution.py:28
  300.4 16.4 %collective-permute-start.7 = (bf16[96,256]{1,0:T(8,128)(2,1)S(1)}, bf16[96,256]{1,0:T(8,128)(2,1)S(1)}, u32[]{:S(2)}, u32[]{:S(2)}) collective-permute-start(bf16[96,256]{1,0:T(8,128)(2,1)S(1)} %fusion.41), channel_id=1, source_target_pairs={{0,256},{256,0},{1,257},{257,1},{2,258},{258,2},{3,259},{259,3},{4... | collective-permute-start | bytes 147464 | tf_op jit(solution)/shard_map/ppermute | solution.py:28
Sparse Core Ops, SparseCore 0:
  10.1 46.1 all-gather.2
  58.4 42.0 all-gather.4

commit v2 on v1

v2 whole, which is shorter than its diff:
```python
import math

import jax
import jax.numpy as jnp
from jax import lax
from jax.sharding import Mesh
from jax.sharding import PartitionSpec as P

root_scale = math.sqrt(2.0 / math.pi)
cubic_term = 0.044715
SWAP = [(0, 1), (1, 0)]
AXES = ("zh", "y", "x", "core", "z4", "z2", "z1")


def gelu_value(hidden):
    curved = jnp.tanh(root_scale * (hidden + cubic_term * hidden * hidden * hidden))
    return 0.5 * hidden * (1.0 + curved)


def gelu_slope(hidden):
    curved = jnp.tanh(root_scale * (hidden + cubic_term * hidden * hidden * hidden))
    return 0.5 * (1.0 + curved) + 0.5 * hidden * (1.0 - curved * curved) * root_scale * (
        1.0 + 3.0 * cubic_term * hidden * hidden
    )


def swap(array, axis):
    return lax.ppermute(array, axis, SWAP)


def flip_if(array, bit, axis):
    return jnp.where(bit == 1, jnp.flip(array, axis), array)


def half_swapped(weights):
    low, high = weights[:, :, :1536], weights[:, :, 1536:]
    bit = lax.axis_index("z1") == 1
    kept, sent = jnp.where(bit, high, low), jnp.where(bit, low, high)
    return jnp.stack([kept, swap(sent, "z1")], 1)


def neighbours(block):
    return tuple(lax.ppermute(block, "x", [(i, i ^ k) for i in range(4)]) for k in (1, 3))


def over_x(block, one, three):
    carried = jnp.where(lax.axis_index("core") == 0, one, three)
    onward = [(i, i ^ (6 if i % 2 == 0 else 2)) for i in range(8)]
    two = lax.ppermute(carried, ("x", "core"), onward)
    return [jnp.concatenate([p[i].reshape(192, -1) for p in (block, one, two, three)], 0) for i in (0, 1)]


def own_order(columns):
    blocks = columns.reshape(columns.shape[:-1] + (2, 2, 64))
    axis = blocks.ndim - 3
    blocks = flip_if(blocks, lax.axis_index("z2"), axis)
    blocks = flip_if(blocks, lax.axis_index("z4"), axis + 1)
    return blocks.reshape(columns.shape)


def over_zh(shards):
    return jnp.stack([shards, swap(shards, "zh")])


def gathered_rows(both):
    sent = jnp.broadcast_to(both[None], (8, 2, 192, 256))
    rows = lax.all_to_all(sent, ("y", "z1"), 0, 0, tiled=True)
    rows = rows.reshape(4, 2, 2, 2, 96, 256).transpose(3, 2, 0, 1, 4, 5)
    rows = flip_if(rows, lax.axis_index("zh"), 1)
    return flip_if(rows, lax.axis_index("z1"), 3)


def core_x_order(blocks):
    x = lax.axis_index("x")
    blocks = flip_if(blocks, x // 2, 0)
    blocks = flip_if(blocks, x % 2, 1)
    return flip_if(blocks, lax.axis_index("core"), 2)


def spread_sum(partial_value):
    total = partial_value
    for name in ("z2", "z4"):
        half = total.shape[0] // 2
        sent = total[half:].astype(jnp.bfloat16)
        total = total[:half].astype(jnp.bfloat16).astype(jnp.float32) + swap(sent, name).astype(jnp.float32)
    return total


def all_tokens(rows):
    for name in ("z4", "z2"):
        rows = jnp.concatenate([rows, swap(rows, name)], 0)
    return rows


def over_y(blocks):
    blocks = flip_if(blocks, lax.axis_index("zh"), 1)
    blocks = flip_if(blocks, lax.axis_index("z1"), 3)
    sent = blocks.transpose(2, 3, 0, 1, 4, 5).reshape(8, 2, 2, 96, 256)
    parts = lax.all_to_all(sent, ("y", "z1"), 0, 0, tiled=True)
    return parts.astype(jnp.float32).sum(0)


def contract(left, right, dims):
    return lax.dot_general(left, right, (dims, ((), ())), preferred_element_type=jnp.float32)


def product(rows, own, other):
    return contract(rows[0], own, ((0,), (0,))) + contract(rows[1], other, ((0,), (0,)))


def back_product(own, other, hidden):
    blocks = jnp.stack([contract(own, hidden, ((1,), (1,))), contract(other, hidden, ((1,), (1,)))])
    blocks = blocks.astype(jnp.bfloat16).reshape(2, 2, 2, 192, 256).transpose(1, 2, 0, 3, 4)
    return core_x_order(blocks).reshape(2, 4, 2, 96, 256)


def local(tokens, up_weight, down_weight, grad_output):
    shards = own_order(jnp.concatenate([tokens.T, grad_output.T], 0))
    halves = half_swapped(jnp.stack([up_weight, down_weight.T]))
    shards, halves = lax.optimization_barrier((shards, halves))
    both = over_zh(shards)
    one, three = neighbours(halves)
    both, one, three = lax.optimization_barrier((both, one, three))
    rows = gathered_rows(both)
    up_own, down_own = over_x(halves, one, three)
    up_other, down_other = swap(up_own, "core"), swap(down_own, "core")
    rows = core_x_order(rows.reshape(2, 2, 2, 2, 192, 256).transpose(1, 2, 3, 0, 4, 5))
    rows = rows.transpose(3, 2, 0, 1, 4, 5).reshape(2, 2, 768, 256)
    hidden = spread_sum(product(rows[0], up_own, up_other))
    activated = all_tokens(gelu_value(hidden).astype(jnp.bfloat16))
    grad_act = spread_sum(product(rows[1], down_own, down_other))
    grad_hidden = all_tokens((grad_act * gelu_slope(hidden)).astype(jnp.bfloat16))
    output = back_product(down_own, down_other, activated)
    grad_tokens = back_product(up_own, up_other, grad_hidden)
    sums = over_y(jnp.stack([output, grad_tokens]))
    other = swap(sums[:, 1].astype(jnp.bfloat16), "zh")
    both = own_order((sums[:, 0] + other.astype(jnp.float32)).astype(jnp.bfloat16))
    return (both[0].T, both[1].T)


def solution(mesh):
    fine = Mesh(mesh.devices.reshape(2, 4, 4, 2, 2, 2, 2), AXES)
    gx, gy, gz = ("zh", "y"), ("x", "core"), ("z4", "z2", "z1")
    in_specs = (P(gy, gz + gx), P(gz + gy, gx), P(gx, gz + gy), P(gy, gz + gx))
    out_specs = (P(gy, gz + gx), P(gy, gz + gx))
    return jax.shard_map(local, mesh=fine, in_specs=in_specs, out_specs=out_specs, check_vma=False)
```

time: 325 us -> 294 us (0.905); the launches traced: 325 us -> 290 us
  waiting for transfers between devices: 189 us -> 134 us
  between operations: 14.6 us -> 1.23 us
  blocking collectives: 14.1 us -> 23.9 us
  starting transfers between devices: 84.7 us -> 94 us
  other arithmetic: 3.11 us -> 12.3 us
  matrix products: 12.7 us -> 16.4 us
    all_gather x2 -> x0, waiting for transfers between devices: 48.5 us -> none  [the longest x1 36.9 us: local(): lax.all_gather(down_weight.T, ('x', 'core'), axis=0, tiled=True)]
    ppermute x15 -> x13, waiting for transfers between devices: 140 us -> 110 us  [swap(): return lax.ppermute(array, axis, SWAP)]
    ppermute x0 -> x3, waiting for transfers between devices: none -> 23.9 us  [the longest x1 17 us: over_x(): two = lax.ppermute(carried, ('x', 'core'), onward)]
    all_to_all x0 -> x1, blocking collectives: none -> 23.9 us  [over_y(): parts = lax.all_to_all(sent, ('y', 'z1'), 0, 0, tiled=True)]
    all_gather x1 -> x0, blocking collectives: 14.1 us -> none  [rows_of(): all_y = lax.all_gather(both.reshape(384, 256), 'y', axis=0, tiled=True)]
    ppermute x0 -> x3, starting transfers between devices: none -> 9.17 us  [the longest x2 6.8 us: neighbours(): lax.ppermute(block, 'x', [(i, i ^ k) for i in range(4)])]
    select_n x10 -> x17, other arithmetic: 0.34 us -> 6.42 us  [the longest x16 5.27 us: flip_if(): return jnp.where(bit == 1, jnp.flip(array, axis), array)]
    ppermute x15 -> x13, starting transfers between devices: 75.1 us -> 79.2 us  [swap(): return lax.ppermute(array, axis, SWAP)]
  transfers between devices with their start and end apart: 19 -> 17, of which waited for: 11 -> 12; matrix products, arithmetic and copies ran while one was open for 6% -> 8% of each run, Pallas kernels for 0% -> 0%
where the time goes in v2:
time: 294 us; the launch traced here: 290 us
  waiting for transfers between devices  134 us (46%)
  starting transfers between devices  94 us (32%)
  blocking collectives  23.9 us (8%)
  matrix products  16.4 us (6%)
  other arithmetic  12.3 us (4%)
  local copies, waits for them, and re-layouts  7.94 us (3%)
    ppermute x13, waiting for transfers between devices, swap(): return lax.ppermute(array, axis, SWAP)  110 us
    ppermute x13, starting transfers between devices, swap(): return lax.ppermute(array, axis, SWAP)  79.2 us
    all_to_all x1, blocking collectives, over_y(): parts = lax.all_to_all(sent, ('y', 'z1'), 0, 0, tiled=True)  23.9 us
    ppermute x1, waiting for transfers between devices, over_x(): two = lax.ppermute(carried, ('x', 'core'), onward)  17 us
    dot_general x8, matrix products, contract(): lax.dot_general(left, right, (dims, ((), ())), preferred_element_type=jnp...  16.4 us
    ppermute x2, waiting for transfers between devices, neighbours(): lax.ppermute(block, 'x', [(i, i ^ k) for i in range(4)])  6.98 us
    ppermute x2, starting transfers between devices, neighbours(): lax.ppermute(block, 'x', [(i, i ^ k) for i in range(4)])  6.8 us
  transfers between devices with their start and end apart: 17, of which 12 were waited for; matrix products, arithmetic and copies ran while one was open for 8% of the time, Pallas kernels for 0%

profile of v2, /device:TPU:24, one launch (start us, length us, event | category | flops | bytes accessed | tf_op | source)
XLA Modules:
  0.0 289.6 jit_solution(12152171966025206775)
XLA Ops:
  2.3 3.8 %collective-permute-start = (bf16[2,96,1536]{2,1,0:T(8,128)(2,1)S(1)}, bf16[2,96,1536]{2,1,0:T(8,128)(2,1)S(1)}, u32[]{:S(2)}, u32[]{:S(2)}) collective-permute-start(bf16[2,96,1536]{2,1,0:T(8,128)(2,1)S(1)} %get-tuple-element.31), channel_id=1, source_target_pairs={{0,1},{1,0},{2,3},{3,2},{4,5},{5,4},{6,7},{7,6},{8,9},{9,8},{10,11... | collective-permute-start | bytes 1769480 | tf_op jit(solution)/shard_map/ppermute | solution.py:28
  6.6 12.9 %collective-permute-done = bf16[2,96,1536]{2,1,0:T(8,128)(2,1)S(1)} collective-permute-done((bf16[2,96,1536]{2,1,0:T(8,128)(2,1)S(1)}, bf16[2,96,1536]{2,1,0:T(8,128)(2,1)S(1)}, u32[]{:S(2)}, u32[]{:S(2)}) %collective-permute-start) | collective-permute-done | bytes 589856 | tf_op jit(solution)/shard_map/ppermute | solution.py:28
  19.6 4.7 %collective-permute-start.3 = (bf16[2,2,96,1536]{3,2,0,1:T(8,128)(2,1)S(1)}, bf16[2,2,96,1536]{3,2,0,1:T(8,128)(2,1)S(1)}, u32[]{:S(2)}, u32[]{:S(2)}) collective-permute-start(bf16[2,2,96,1536]{3,2,0,1:T(8,128)(2,1)S(1)} %pad_maximum_fusion.3), channel_id=1, source_target_pairs={{0,48},{16,32},{32,16},{48,0},{1,49},{17,33},{33,17},{49,1},{2,50}... | collective-permute-start | bytes 3538952 | tf_op jit(solution)/shard_map/ppermute | solution.py:43
  26.4 15.5 %collective-permute-start.1 = (bf16[192,256]{0,1:T(8,128)(2,1)S(1)}, bf16[192,256]{0,1:T(8,128)(2,1)S(1)}, u32[]{:S(2)}, u32[]{:S(2)}) collective-permute-start(bf16[192,256]{0,1:T(8,128)(2,1)S(1)} %bitcast.102), channel_id=1, source_target_pairs={{0,256},{256,0},{1,257},{257,1},{2,258},{258,2},{3,259},{259,3},{4... | collective-permute-start | bytes 294920 | tf_op jit(solution)/shard_map/ppermute | solution.py:28
  42.0 3.2 %collective-permute-done.1 = bf16[192,256]{0,1:T(8,128)(2,1)S(1)} collective-permute-done((bf16[192,256]{0,1:T(8,128)(2,1)S(1)}, bf16[192,256]{0,1:T(8,128)(2,1)S(1)}, u32[]{:S(2)}, u32[]{:S(2)}) %collective-permute-start.1) | collective-permute-done | bytes 98336 | tf_op jit(solution)/shard_map/ppermute | solution.py:28
  45.9 3.8 %collective-permute-done.3 = bf16[2,2,96,1536]{3,2,0,1:T(8,128)(2,1)S(1)} collective-permute-done((bf16[2,2,96,1536]{3,2,0,1:T(8,128)(2,1)S(1)}, bf16[2,2,96,1536]{3,2,0,1:T(8,128)(2,1)S(1)}, u32[]{:S(2)}, u32[]{:S(2)}) %collective-permute-start.3) | collective-permute-done | bytes 1179680 | tf_op jit(solution)/shard_map/ppermute | solution.py:43
  49.7 3.2 %collective-permute-done.2 = bf16[2,2,96,1536]{3,2,0,1:T(8,128)(2,1)S(1)} collective-permute-done((bf16[2,2,96,1536]{3,2,0,1:T(8,128)(2,1)S(1)}, bf16[2,2,96,1536]{3,2,0,1:T(8,128)(2,1)S(1)}, u32[]{:S(2)}, u32[]{:S(2)}) %collective-permute-start.2) | collective-permute-done | bytes 1179680 | tf_op jit(solution)/shard_map/ppermute | solution.py:43
  57.0 5.7 %all-to-all-start = ((bf16[8,2,192,256]{3,2,1,0:T(8,128)(2,1)}), bf16[8,2,192,256]{3,2,1,0:T(8,128)(2,1)}, u32[]{:S(2)}, u32[]{:S(2)}) async-start(bf16[8,2,192,256]{3,2,1,0:T(8,128)(2,1)} %broadcast_in_dim.2), calls=%async_computation | async-start | bytes 3145728 | tf_op jit(solution)/shard_map/all_to_all | solution.py:67
  63.8 2.4 collective-permute-start.4
  66.5 17.0 %collective-permute-done.4 = bf16[2,2,96,1536]{3,2,0,1:T(8,128)(2,1)} collective-permute-done((bf16[2,2,96,1536]{3,2,0,1:T(8,128)(2,1)}, bf16[2,2,96,1536]{3,2,0,1:T(8,128)(2,1)}, u32[]{:S(2)}, u32[]{:S(2)}) %collective-permute-start.4) | collective-permute-done | bytes 1179680 | tf_op jit(solution)/shard_map/ppermute | solution.py:49
  88.4 2.4 collective-permute-start.10
  90.8 2.5 reverse_select_fusion.6
  95.9 2.5 fusion
  98.4 5.2 %collective-permute-start.6 = (bf16[128,1536]{1,0:T(8,128)(2,1)S(1)}, bf16[128,1536]{1,0:T(8,128)(2,1)S(1)}, u32[]{:S(2)}, u32[]{:S(2)}) collective-permute-start(bf16[128,1536]{1,0:T(8,128)(2,1)S(1)} %slice.134), channel_id=1, source_target_pairs={{0,2},{2,0},{1,3},{3,1},{4,6},{6,4},{5,7},{7,5},{8,10},{10,8},{9,1... | collective-permute-start | bytes 1179656 | tf_op jit(solution)/shard_map/ppermute | solution.py:28
  103.6 2.5 fusion.25
  106.0 2.5 fusion.1
  110.5 19.9 %collective-permute-done.6 = bf16[128,1536]{1,0:T(8,128)(2,1)S(1)} collective-permute-done((bf16[128,1536]{1,0:T(8,128)(2,1)S(1)}, bf16[128,1536]{1,0:T(8,128)(2,1)S(1)}, u32[]{:S(2)}, u32[]{:S(2)}) %collective-permute-start.6) | collective-permute-done | bytes 393248 | tf_op jit(solution)/shard_map/ppermute | solution.py:28
  130.4 9.1 %collective-permute-start.7 = (bf16[64,1536]{1,0:T(8,128)(2,1)S(1)}, bf16[64,1536]{1,0:T(8,128)(2,1)S(1)}, u32[]{:S(2)}, u32[]{:S(2)}) collective-permute-start(bf16[64,1536]{1,0:T(8,128)(2,1)S(1)} %slice.136), channel_id=1, source_target_pairs={{0,4},{4,0},{1,5},{5,1},{2,6},{6,2},{3,7},{7,3},{8,12},{12,8},{9,1... | collective-permute-start | bytes 589832 | tf_op jit(solution)/shard_map/ppermute | solution.py:28
  139.7 12.6 %collective-permute-start.12 = (bf16[64,1536]{1,0:T(8,128)(2,1)S(1)}, bf16[64,1536]{1,0:T(8,128)(2,1)S(1)}, u32[]{:S(2)}, u32[]{:S(2)}) collective-permute-start(bf16[64,1536]{1,0:T(8,128)(2,1)S(1)} %slice.142), channel_id=1, source_target_pairs={{0,4},{4,0},{1,5},{5,1},{2,6},{6,2},{3,7},{7,3},{8,12},{12,8},{9,1... | collective-permute-start | bytes 589832 | tf_op jit(solution)/shard_map/ppermute | solution.py:28
  152.3 26.2 %collective-permute-done.12 = bf16[64,1536]{1,0:T(8,128)(2,1)S(1)} collective-permute-done((bf16[64,1536]{1,0:T(8,128)(2,1)S(1)}, bf16[64,1536]{1,0:T(8,128)(2,1)S(1)}, u32[]{:S(2)}, u32[]{:S(2)}) %collective-permute-start.12) | collective-permute-done | bytes 196640 | tf_op jit(solution)/shard_map/ppermute | solution.py:28
  180.8 7.8 %collective-permute-start.13 = (bf16[64,1536]{1,0:T(8,128)(2,1)S(1)}, bf16[64,1536]{1,0:T(8,128)(2,1)S(1)}, u32[]{:S(2)}, u32[]{:S(2)}) collective-permute-start(bf16[64,1536]{1,0:T(8,128)(2,1)S(1)} %get-tuple-element.33), channel_id=1, source_target_pairs={{0,4},{4,0},{1,5},{5,1},{2,6},{6,2},{3,7},{7,3},{8,12},{12,8},{9,1... | collective-permute-start | bytes 589832 | tf_op jit(solution)/shard_map/ppermute | solution.py:28
  188.6 15.6 %collective-permute-done.8 = bf16[64,1536]{1,0:T(8,128)(2,1)S(1)} collective-permute-done((bf16[64,1536]{1,0:T(8,128)(2,1)S(1)}, bf16[64,1536]{1,0:T(8,128)(2,1)S(1)}, u32[]{:S(2)}, u32[]{:S(2)}) %collective-permute-start.8) | collective-permute-done | bytes 196640 | tf_op jit(solution)/shard_map/ppermute | solution.py:28
  206.1 2.4 collective-permute-done.13
  208.5 2.7 collective-permute-start.14
  211.2 22.6 %collective-permute-done.9 = bf16[128,1536]{1,0:T(8,128)(2,1)S(1)} collective-permute-done((bf16[128,1536]{1,0:T(8,128)(2,1)S(1)}, bf16[128,1536]{1,0:T(8,128)(2,1)S(1)}, u32[]{:S(2)}, u32[]{:S(2)}) %collective-permute-start.9) | collective-permute-done | bytes 393248 | tf_op jit(solution)/shard_map/ppermute | solution.py:28
  233.7 2.5 convolution_convert_fusion.2
  236.2 2.5 convolution_convert_fusion.3
  239.2 2.9 collective-permute-done.14
  242.1 2.5 convolution_convert_fusion
  246.9 23.9 %all_to_all.10 = bf16[8,2,2,96,256]{4,3,1,2,0:T(8,128)(2,1)S(1)} all-to-all(bf16[8,2,2,96,256]{4,3,1,2,0:T(8,128)(2,1)S(1)} %bitcast.81), channel_id=1, replica_groups=mesh['zh'=2,'y'=4,'x'=4,'core'=2,'z4'=2,'z2'=2,'z1'=2] {'y','z1'}, dimensions={0} | all-to-all | bytes 3145728 | tf_op jit(solution)/shard_map/all_to_all | solution.py:99
  271.0 12.4 %collective-permute-start.15 = (bf16[2,96,256]{2,1,0:T(8,128)(2,1)S(1)}, bf16[2,96,256]{2,1,0:T(8,128)(2,1)S(1)}, u32[]{:S(2)}, u32[]{:S(2)}) collective-permute-start(bf16[2,96,256]{2,1,0:T(8,128)(2,1)S(1)} %fusion.13), channel_id=1, source_target_pairs={{0,256},{256,0},{1,257},{257,1},{2,258},{258,2},{3,259},{259,3},{4... | collective-permute-start | bytes 294920 | tf_op jit(solution)/shard_map/ppermute | solution.py:28
  283.4 4.5 %collective-permute-done.15 = bf16[2,96,256]{2,1,0:T(8,128)(2,1)S(1)} collective-permute-done((bf16[2,96,256]{2,1,0:T(8,128)(2,1)S(1)}, bf16[2,96,256]{2,1,0:T(8,128)(2,1)S(1)}, u32[]{:S(2)}, u32[]{:S(2)}) %collective-permute-start.15) | collective-permute-done | bytes 98336 | tf_op jit(solution)/shard_map/ppermute | solution.py:28
  (68 shorter events, 29.1 us)
Async XLA Ops:
  0.6 5.5 %copy-start = (bf16[256,96]{0,1:T(8,128)(2,1)S(1)}, bf16[256,96]{0,1:T(8,128)(2,1)}, u32[]{:S(2)}) copy-start(bf16[256,96]{0,1:T(8,128)(2,1)} %param.4) | copy-start | bytes 147460
  0.6 5.7 %copy-start.1 = (bf16[256,96]{0,1:T(8,128)(2,1)S(1)}, bf16[256,96]{0,1:T(8,128)(2,1)}, u32[]{:S(2)}) copy-start(bf16[256,96]{0,1:T(8,128)(2,1)} %param.7) | copy-start | bytes 147460
  2.3 17.1 %collective-permute-start = (bf16[2,96,1536]{2,1,0:T(8,128)(2,1)S(1)}, bf16[2,96,1536]{2,1,0:T(8,128)(2,1)S(1)}, u32[]{:S(2)}, u32[]{:S(2)}) collective-permute-start(bf16[2,96,1536]{2,1,0:T(8,128)(2,1)S(1)} %get-tuple-element.31), channel_id=1, source_target_pairs={{0,1},{1,0},{2,3},{3,2},{4,5},{5,4},{6,7},{7,6},{8,9},{9,8},{10,11... | collective-permute-start | bytes 1769480 | tf_op jit(solution)/shard_map/ppermute | solution.py:28
  19.6 30.1 %collective-permute-start.3 = (bf16[2,2,96,1536]{3,2,0,1:T(8,128)(2,1)S(1)}, bf16[2,2,96,1536]{3,2,0,1:T(8,128)(2,1)S(1)}, u32[]{:S(2)}, u32[]{:S(2)}) collective-permute-start(bf16[2,2,96,1536]{3,2,0,1:T(8,128)(2,1)S(1)} %pad_maximum_fusion.3), channel_id=1, source_target_pairs={{0,48},{16,32},{32,16},{48,0},{1,49},{17,33},{33,17},{49,1},{2,50}... | collective-permute-start | bytes 3538952 | tf_op jit(solution)/shard_map/ppermute | solution.py:43
  24.3 28.7 %collective-permute-start.2 = (bf16[2,2,96,1536]{3,2,0,1:T(8,128)(2,1)S(1)}, bf16[2,2,96,1536]{3,2,0,1:T(8,128)(2,1)S(1)}, u32[]{:S(2)}, u32[]{:S(2)}) collective-permute-start(bf16[2,2,96,1536]{3,2,0,1:T(8,128)(2,1)S(1)} %pad_maximum_fusion.3), channel_id=1, source_target_pairs={{0,16},{16,0},{32,48},{48,32},{1,17},{17,1},{33,49},{49,33},{2,18}... | collective-permute-start | bytes 3538952 | tf_op jit(solution)/shard_map/ppermute | solution.py:43
  26.4 18.8 %collective-permute-start.1 = (bf16[192,256]{0,1:T(8,128)(2,1)S(1)}, bf16[192,256]{0,1:T(8,128)(2,1)S(1)}, u32[]{:S(2)}, u32[]{:S(2)}) collective-permute-start(bf16[192,256]{0,1:T(8,128)(2,1)S(1)} %bitcast.102), channel_id=1, source_target_pairs={{0,256},{256,0},{1,257},{257,1},{2,258},{258,2},{3,259},{259,3},{4... | collective-permute-start | bytes 294920 | tf_op jit(solution)/shard_map/ppermute | solution.py:28
  57.0 33.8 %all-to-all-start = ((bf16[8,2,192,256]{3,2,1,0:T(8,128)(2,1)}), bf16[8,2,192,256]{3,2,1,0:T(8,128)(2,1)}, u32[]{:S(2)}, u32[]{:S(2)}) async-start(bf16[8,2,192,256]{3,2,1,0:T(8,128)(2,1)} %broadcast_in_dim.2), calls=%async_computation | async-start | bytes 3145728 | tf_op jit(solution)/shard_map/all_to_all | solution.py:67
  63.8 19.6 %collective-permute-start.4 = (bf16[2,2,96,1536]{3,2,0,1:T(8,128)(2,1)}, bf16[2,2,96,1536]{3,2,0,1:T(8,128)(2,1)}, u32[]{:S(2)}, u32[]{:S(2)}) collective-permute-start(bf16[2,2,96,1536]{3,2,0,1:T(8,128)(2,1)} %broadcast_select_fusion), channel_id=1, source_target_pairs={{0,48},{8,24},{16,32},{24,8},{32,16},{40,56},{48,0},{56,40},{1,49}... | collective-permute-start | bytes 3538952 | tf_op jit(solution)/shard_map/ppermute | solution.py:49
  84.9 11.0 %collective-permute-start.5 = (bf16[768,1536]{1,0:T(8,128)(2,1)S(1)}, bf16[768,1536]{1,0:T(8,128)(2,1)}, u32[]{:S(2)}, u32[]{:S(2)}) collective-permute-start(bf16[768,1536]{1,0:T(8,128)(2,1)S(1)} %pad_maximum_fusion.1), channel_id=1, source_target_pairs={{0,8},{8,0},{1,9},{9,1},{2,10},{10,2},{3,11},{11,3},{4,12},{12,4},... | collective-permute-start | bytes 7077896 | tf_op jit(solution)/shard_map/ppermute | solution.py:28
  88.4 17.6 %collective-permute-start.10 = (bf16[768,1536]{1,0:T(8,128)(2,1)}, bf16[768,1536]{1,0:T(8,128)(2,1)}, u32[]{:S(2)}, u32[]{:S(2)}) collective-permute-start(bf16[768,1536]{1,0:T(8,128)(2,1)} %pad_maximum_fusion), channel_id=1, source_target_pairs={{0,8},{8,0},{1,9},{9,1},{2,10},{10,2},{3,11},{11,3},{4,12},{12,4},... | collective-permute-start | bytes 7077896 | tf_op jit(solution)/shard_map/ppermute | solution.py:28
  98.4 31.9 %collective-permute-start.6 = (bf16[128,1536]{1,0:T(8,128)(2,1)S(1)}, bf16[128,1536]{1,0:T(8,128)(2,1)S(1)}, u32[]{:S(2)}, u32[]{:S(2)}) collective-permute-start(bf16[128,1536]{1,0:T(8,128)(2,1)S(1)} %slice.134), channel_id=1, source_target_pairs={{0,2},{2,0},{1,3},{3,1},{4,6},{6,4},{5,7},{7,5},{8,10},{10,8},{9,1... | collective-permute-start | bytes 1179656 | tf_op jit(solution)/shard_map/ppermute | solution.py:28
  108.5 31.0 %collective-permute-start.11 = (bf16[128,1536]{1,0:T(8,128)(2,1)S(1)}, bf16[128,1536]{1,0:T(8,128)(2,1)S(1)}, u32[]{:S(2)}, u32[]{:S(2)}) collective-permute-start(bf16[128,1536]{1,0:T(8,128)(2,1)S(1)} %slice.140), channel_id=1, source_target_pairs={{0,2},{2,0},{1,3},{3,1},{4,6},{6,4},{5,7},{7,5},{8,10},{10,8},{9,1... | collective-permute-start | bytes 1179656 | tf_op jit(solution)/shard_map/ppermute | solution.py:28
  130.4 21.8 %collective-permute-start.7 = (bf16[64,1536]{1,0:T(8,128)(2,1)S(1)}, bf16[64,1536]{1,0:T(8,128)(2,1)S(1)}, u32[]{:S(2)}, u32[]{:S(2)}) collective-permute-start(bf16[64,1536]{1,0:T(8,128)(2,1)S(1)} %slice.136), channel_id=1, source_target_pairs={{0,4},{4,0},{1,5},{5,1},{2,6},{6,2},{3,7},{7,3},{8,12},{12,8},{9,1... | collective-permute-start | bytes 589832 | tf_op jit(solution)/shard_map/ppermute | solution.py:28
  139.7 38.8 %collective-permute-start.12 = (bf16[64,1536]{1,0:T(8,128)(2,1)S(1)}, bf16[64,1536]{1,0:T(8,128)(2,1)S(1)}, u32[]{:S(2)}, u32[]{:S(2)}) collective-permute-start(bf16[64,1536]{1,0:T(8,128)(2,1)S(1)} %slice.142), channel_id=1, source_target_pairs={{0,4},{4,0},{1,5},{5,1},{2,6},{6,2},{3,7},{7,3},{8,12},{12,8},{9,1... | collective-permute-start | bytes 589832 | tf_op jit(solution)/shard_map/ppermute | solution.py:28
  178.8 25.3 %collective-permute-start.8 = (bf16[64,1536]{1,0:T(8,128)(2,1)S(1)}, bf16[64,1536]{1,0:T(8,128)(2,1)S(1)}, u32[]{:S(2)}, u32[]{:S(2)}) collective-permute-start(bf16[64,1536]{1,0:T(8,128)(2,1)S(1)} %get-tuple-element.32), channel_id=1, source_target_pairs={{0,4},{4,0},{1,5},{5,1},{2,6},{6,2},{3,7},{7,3},{8,12},{12,8},{9,1... | collective-permute-start | bytes 589832 | tf_op jit(solution)/shard_map/ppermute | solution.py:28
  180.8 27.7 %collective-permute-start.13 = (bf16[64,1536]{1,0:T(8,128)(2,1)S(1)}, bf16[64,1536]{1,0:T(8,128)(2,1)S(1)}, u32[]{:S(2)}, u32[]{:S(2)}) collective-permute-start(bf16[64,1536]{1,0:T(8,128)(2,1)S(1)} %get-tuple-element.33), channel_id=1, source_target_pairs={{0,4},{4,0},{1,5},{5,1},{2,6},{6,2},{3,7},{7,3},{8,12},{12,8},{9,1... | collective-permute-start | bytes 589832 | tf_op jit(solution)/shard_map/ppermute | solution.py:28
  204.2 29.5 %collective-permute-start.9 = (bf16[128,1536]{1,0:T(8,128)(2,1)S(1)}, bf16[128,1536]{1,0:T(8,128)(2,1)S(1)}, u32[]{:S(2)}, u32[]{:S(2)}) collective-permute-start(bf16[128,1536]{1,0:T(8,128)(2,1)S(1)} %pad_maximum_fusion.7), channel_id=1, source_target_pairs={{0,2},{2,0},{1,3},{3,1},{4,6},{6,4},{5,7},{7,5},{8,10},{10,8},{9,1... | collective-permute-start | bytes 1179656 | tf_op jit(solution)/shard_map/ppermute | solution.py:28
  208.5 33.6 %collective-permute-start.14 = (bf16[128,1536]{1,0:T(8,128)(2,1)S(1)}, bf16[128,1536]{1,0:T(8,128)(2,1)S(1)}, u32[]{:S(2)}, u32[]{:S(2)}) collective-permute-start(bf16[128,1536]{1,0:T(8,128)(2,1)S(1)} %pad_maximum_fusion.8), channel_id=1, source_target_pairs={{0,2},{2,0},{1,3},{3,1},{4,6},{6,4},{5,7},{7,5},{8,10},{10,8},{9,1... | collective-permute-start | bytes 1179656 | tf_op jit(solution)/shard_map/ppermute | solution.py:28
  271.0 16.9 %collective-permute-start.15 = (bf16[2,96,256]{2,1,0:T(8,128)(2,1)S(1)}, bf16[2,96,256]{2,1,0:T(8,128)(2,1)S(1)}, u32[]{:S(2)}, u32[]{:S(2)}) collective-permute-start(bf16[2,96,256]{2,1,0:T(8,128)(2,1)S(1)} %fusion.13), channel_id=1, source_target_pairs={{0,256},{256,0},{1,257},{257,1},{2,258},{258,2},{3,259},{259,3},{4... | collective-permute-start | bytes 294920 | tf_op jit(solution)/shard_map/ppermute | solution.py:28

commit v3 on v2

--- a/solution.py
+++ b/solution.py
@@ -32,11 +32,11 @@
     return jnp.where(bit == 1, jnp.flip(array, axis), array)
 
 
-def half_swapped(weights):
-    low, high = weights[:, :, :1536], weights[:, :, 1536:]
-    bit = lax.axis_index("z1") == 1
+def half_swapped(weight):
+    low, high = weight[:, :1536], weight[:, 1536:]
+    bit = lax.axis_index("z4") == 1
     kept, sent = jnp.where(bit, high, low), jnp.where(bit, low, high)
-    return jnp.stack([kept, swap(sent, "z1")], 1)
+    return jnp.concatenate([kept, swap(sent, "z4")], 0)
 
 
 def neighbours(block):
@@ -47,14 +47,14 @@
     carried = jnp.where(lax.axis_index("core") == 0, one, three)
     onward = [(i, i ^ (6 if i % 2 == 0 else 2)) for i in range(8)]
     two = lax.ppermute(carried, ("x", "core"), onward)
-    return [jnp.concatenate([p[i].reshape(192, -1) for p in (block, one, two, three)], 0) for i in (0, 1)]
+    return jnp.concatenate([block, one, two, three], 0)
 
 
 def own_order(columns):
     blocks = columns.reshape(columns.shape[:-1] + (2, 2, 64))
     axis = blocks.ndim - 3
-    blocks = flip_if(blocks, lax.axis_index("z2"), axis)
-    blocks = flip_if(blocks, lax.axis_index("z4"), axis + 1)
+    blocks = flip_if(blocks, lax.axis_index("z1"), axis)
+    blocks = flip_if(blocks, lax.axis_index("z2"), axis + 1)
     return blocks.reshape(columns.shape)
 
 
@@ -62,12 +62,15 @@
     return jnp.stack([shards, swap(shards, "zh")])
 
 
-def gathered_rows(both):
-    sent = jnp.broadcast_to(both[None], (8, 2, 192, 256))
-    rows = lax.all_to_all(sent, ("y", "z1"), 0, 0, tiled=True)
+def with_partner(both):
+    return jnp.stack([both, swap(both, "z4")])
+
+
+def gathered_rows(quad):
+    sent = jnp.broadcast_to(quad.reshape(1, 768, 256), (4, 768, 256)).reshape(3072, 256)
+    rows = lax.all_to_all(sent, "y", 0, 0, tiled=True)
     rows = rows.reshape(4, 2, 2, 2, 96, 256).transpose(3, 2, 0, 1, 4, 5)
-    rows = flip_if(rows, lax.axis_index("zh"), 1)
-    return flip_if(rows, lax.axis_index("z1"), 3)
+    return flip_if(rows, lax.axis_index("zh"), 1)
 
 
 def core_x_order(blocks):
@@ -79,7 +82,7 @@
 
 def spread_sum(partial_value):
     total = partial_value
-    for name in ("z2", "z4"):
+    for name in ("z1", "z2"):
         half = total.shape[0] // 2
         sent = total[half:].astype(jnp.bfloat16)
         total = total[:half].astype(jnp.bfloat16).astype(jnp.float32) + swap(sent, name).astype(jnp.float32)
@@ -87,17 +90,19 @@
 
 
 def all_tokens(rows):
-    for name in ("z4", "z2"):
+    for name in ("z2", "z1"):
         rows = jnp.concatenate([rows, swap(rows, name)], 0)
     return rows
 
 
-def over_y(blocks):
+def over_gx(blocks):
     blocks = flip_if(blocks, lax.axis_index("zh"), 1)
-    blocks = flip_if(blocks, lax.axis_index("z1"), 3)
-    sent = blocks.transpose(2, 3, 0, 1, 4, 5).reshape(8, 2, 2, 96, 256)
-    parts = lax.all_to_all(sent, ("y", "z1"), 0, 0, tiled=True)
-    return parts.astype(jnp.float32).sum(0)
+    sent = blocks.transpose(2, 3, 1, 0, 4, 5).reshape(3072, 256)
+    parts = lax.all_to_all(sent, "y", 0, 0, tiled=True)
+    total = parts.reshape(4, 2, 2, 2, 96, 256).astype(jnp.float32).sum(0)
+    total = total[0] + swap(total[1].astype(jnp.bfloat16), "z4").astype(jnp.float32)
+    total = total[0] + swap(total[1].astype(jnp.bfloat16), "zh").astype(jnp.float32)
+    return total.astype(jnp.bfloat16)
 
 
 def contract(left, right, dims):
@@ -116,13 +121,12 @@
 
 def local(tokens, up_weight, down_weight, grad_output):
     shards = own_order(jnp.concatenate([tokens.T, grad_output.T], 0))
-    halves = half_swapped(jnp.stack([up_weight, down_weight.T]))
-    shards, halves = lax.optimization_barrier((shards, halves))
-    both = over_zh(shards)
-    one, three = neighbours(halves)
-    both, one, three = lax.optimization_barrier((both, one, three))
-    rows = gathered_rows(both)
-    up_own, down_own = over_x(halves, one, three)
+    up_half, down_half = half_swapped(up_weight), half_swapped(down_weight.T)
+    quad = with_partner(over_zh(shards))
+    quad, up_half, down_half = lax.optimization_barrier((quad, up_half, down_half))
+    near = neighbours(up_half) + neighbours(down_half)
+    rows = gathered_rows(quad)
+    up_own, down_own = over_x(up_half, *near[:2]), over_x(down_half, *near[2:])
     up_other, down_other = swap(up_own, "core"), swap(down_own, "core")
     rows = core_x_order(rows.reshape(2, 2, 2, 2, 192, 256).transpose(1, 2, 3, 0, 4, 5))
     rows = rows.transpose(3, 2, 0, 1, 4, 5).reshape(2, 2, 768, 256)
@@ -132,9 +136,7 @@
     grad_hidden = all_tokens((grad_act * gelu_slope(hidden)).astype(jnp.bfloat16))
     output = back_product(down_own, down_other, activated)
     grad_tokens = back_product(up_own, up_other, grad_hidden)
-    sums = over_y(jnp.stack([output, grad_tokens]))
-    other = swap(sums[:, 1].astype(jnp.bfloat16), "zh")
-    both = own_order((sums[:, 0] + other.astype(jnp.float32)).astype(jnp.bfloat16))
+    both = own_order(over_gx(jnp.stack([output, grad_tokens])))
     return (both[0].T, both[1].T)
 
 

time: 294 us -> 314 us (1.068)
  waiting for transfers between devices: 134 us -> 158 us
  starting transfers between devices: 94 us -> 88.5 us
  local copies, waits for them, and re-layouts: 7.94 us -> 11.7 us
  matrix products: 16.4 us -> 19.7 us
    ppermute x13 -> x16, waiting for transfers between devices: 110 us -> 143 us  [swap(): return lax.ppermute(array, axis, SWAP)]
    ppermute x13 -> x16, starting transfers between devices: 79.2 us -> 65.4 us  [swap(): return lax.ppermute(array, axis, SWAP)]
    ppermute x1 -> x2, waiting for transfers between devices: 17 us -> 4.6 us  [over_x(): two = lax.ppermute(carried, ('x', 'core'), onward)]
    unnamed x8 -> x10, local copies, waits for them, and re-layouts: 1.68 us -> 7.85 us
    ppermute x2 -> x4, starting transfers between devices: 6.8 us -> 12.4 us  [neighbours(): lax.ppermute(block, 'x', [(i, i ^ k) for i in range(4)])]
    ppermute x1 -> x2, starting transfers between devices: 2.38 us -> 6.03 us  [over_x(): two = lax.ppermute(carried, ('x', 'core'), onward)]
    ppermute x2 -> x4, waiting for transfers between devices: 6.98 us -> 10.6 us  [neighbours(): lax.ppermute(block, 'x', [(i, i ^ k) for i in range(4)])]
    dot_general x8, matrix products: 16.4 us -> 19.7 us  [contract(): lax.dot_general(left, right, (dims, ((), ())), preferred_element_type=jnp...]
  transfers between devices with their start and end apart: 17 -> 23, of which waited for: 12 -> 16; matrix products, arithmetic and copies ran while one was open for 8% -> 10% of each run, Pallas kernels for 0% -> 0%
where the time goes in v3:
time: 314 us; the launch traced here: 312 us
  waiting for transfers between devices  158 us (50%)
  starting transfers between devices  88.5 us (28%)
  blocking collectives  22.4 us (7%)
  matrix products  19.7 us (6%)
  local copies, waits for them, and re-layouts  11.7 us (4%)
  other arithmetic  9.72 us (3%)
    ppermute x16, waiting for transfers between devices, swap(): return lax.ppermute(array, axis, SWAP)  143 us
    ppermute x16, starting transfers between devices, swap(): return lax.ppermute(array, axis, SWAP)  65.4 us
    all_to_all x1, blocking collectives, over_gx(): parts = lax.all_to_all(sent, 'y', 0, 0, tiled=True)  22.4 us
    dot_general x8, matrix products, contract(): lax.dot_general(left, right, (dims, ((), ())), preferred_element_type=jnp...  19.7 us
    ppermute x4, starting transfers between devices, neighbours(): lax.ppermute(block, 'x', [(i, i ^ k) for i in range(4)])  12.4 us
    ppermute x4, waiting for transfers between devices, neighbours(): lax.ppermute(block, 'x', [(i, i ^ k) for i in range(4)])  10.6 us
    unnamed x10, local copies, waits for them, and re-layouts  7.85 us
  transfers between devices with their start and end apart: 23, of which 16 were waited for; matrix products, arithmetic and copies ran while one was open for 10% of the time, Pallas kernels for 0%

profile of v3, /device:TPU:24, one launch (start us, length us, event | category | flops | bytes accessed | tf_op | source)
XLA Modules:
  0.0 311.6 jit_solution(12878677263058639097)
XLA Ops:
  2.7 15.7 %collective-permute-start = (bf16[192,256]{0,1:T(8,128)(2,1)S(1)}, bf16[192,256]{0,1:T(8,128)(2,1)S(1)}, u32[]{:S(2)}, u32[]{:S(2)}) collective-permute-start(bf16[192,256]{0,1:T(8,128)(2,1)S(1)} %bitcast.87), channel_id=1, source_target_pairs={{0,256},{256,0},{1,257},{257,1},{2,258},{258,2},{3,259},{259,3},{4... | collective-permute-start | bytes 294920 | tf_op jit(solution)/shard_map/ppermute | solution.py:28
  19.6 4.3 %collective-permute-start.2 = (bf16[96,1536]{1,0:T(8,128)(2,1)S(1)}, bf16[96,1536]{1,0:T(8,128)(2,1)S(1)}, u32[]{:S(2)}, u32[]{:S(2)}) collective-permute-start(bf16[96,1536]{1,0:T(8,128)(2,1)S(1)} %get-tuple-element.25), channel_id=1, source_target_pairs={{0,4},{4,0},{1,5},{5,1},{2,6},{6,2},{3,7},{7,3},{8,12},{12,8},{9,1... | collective-permute-start | bytes 884744 | tf_op jit(solution)/shard_map/ppermute | solution.py:28
  23.9 11.0 %collective-permute-start.1 = (bf16[2,192,256]{1,2,0:T(8,128)(2,1)S(1)}, bf16[2,192,256]{1,2,0:T(8,128)(2,1)S(1)}, u32[]{:S(2)}, u32[]{:S(2)}) collective-permute-start(bf16[2,192,256]{1,2,0:T(8,128)(2,1)S(1)} %get-tuple-element.27), channel_id=1, source_target_pairs={{0,4},{4,0},{1,5},{5,1},{2,6},{6,2},{3,7},{7,3},{8,12},{12,8},{9,1... | collective-permute-start | bytes 589832 | tf_op jit(solution)/shard_map/ppermute | solution.py:28
  37.0 60.7 %collective-permute-done.1 = bf16[2,192,256]{1,2,0:T(8,128)(2,1)S(1)} collective-permute-done((bf16[2,192,256]{1,2,0:T(8,128)(2,1)S(1)}, bf16[2,192,256]{1,2,0:T(8,128)(2,1)S(1)}, u32[]{:S(2)}, u32[]{:S(2)}) %collective-permute-start.1) | collective-permute-done | bytes 196640 | tf_op jit(solution)/shard_map/ppermute | solution.py:28
  97.8 6.1 %collective-permute-done.3 = bf16[96,1536]{1,0:T(8,128)(2,1)S(1)} collective-permute-done((bf16[96,1536]{1,0:T(8,128)(2,1)S(1)}, bf16[96,1536]{1,0:T(8,128)(2,1)S(1)}, u32[]{:S(2)}, u32[]{:S(2)}) %collective-permute-start.3) | collective-permute-done | bytes 294944 | tf_op jit(solution)/shard_map/ppermute | solution.py:28
  103.9 4.7 %collective-permute-start.8 = (bf16[192,1536]{1,0:T(8,128)(2,1)S(1)}, bf16[192,1536]{1,0:T(8,128)(2,1)S(1)}, u32[]{:S(2)}, u32[]{:S(2)}) collective-permute-start(bf16[192,1536]{1,0:T(8,128)(2,1)S(1)} %pad_maximum_fusion.3), channel_id=1, source_target_pairs={{0,48},{16,32},{32,16},{48,0},{1,49},{17,33},{33,17},{49,1},{2,50}... | collective-permute-start | bytes 1769480 | tf_op jit(solution)/shard_map/ppermute | solution.py:43
  110.8 3.0 collective-permute-start.5
  113.8 2.6 collective-permute-start.4
  117.3 6.0 %collective-permute-done.8 = bf16[192,1536]{1,0:T(8,128)(2,1)S(1)} collective-permute-done((bf16[192,1536]{1,0:T(8,128)(2,1)S(1)}, bf16[192,1536]{1,0:T(8,128)(2,1)S(1)}, u32[]{:S(2)}, u32[]{:S(2)}) %collective-permute-start.8) | collective-permute-done | bytes 589856 | tf_op jit(solution)/shard_map/ppermute | solution.py:43
  123.2 3.6 %collective-permute-done.7 = bf16[192,1536]{1,0:T(8,128)(2,1)} collective-permute-done((bf16[192,1536]{1,0:T(8,128)(2,1)S(1)}, bf16[192,1536]{1,0:T(8,128)(2,1)}, u32[]{:S(2)}, u32[]{:S(2)}) %collective-permute-start.7) | collective-permute-done | bytes 589856 | tf_op jit(solution)/shard_map/ppermute | solution.py:43
  133.8 4.7 %all-to-all-start = ((bf16[4,768,256]{2,1,0:T(8,128)(2,1)}), bf16[4,768,256]{2,1,0:T(8,128)(2,1)S(1)}, u32[]{:S(2)}, u32[]{:S(2)}) async-start(bf16[4,768,256]{2,1,0:T(8,128)(2,1)} %broadcast_in_dim.8), calls=%async_computation | async-start | bytes 3145728 | tf_op jit(solution)/shard_map/all_to_all | solution.py:71
  141.5 3.7 %collective-permute-start.6 = (bf16[192,1536]{1,0:T(8,128)(2,1)S(1)}, bf16[192,1536]{1,0:T(8,128)(2,1)S(1)}, u32[]{:S(2)}, u32[]{:S(2)}) collective-permute-start(bf16[192,1536]{1,0:T(8,128)(2,1)S(1)} %get-tuple-element.18), channel_id=1, source_target_pairs={{0,48},{8,24},{16,32},{24,8},{32,16},{40,56},{48,0},{56,40},{1,49}... | collective-permute-start | bytes 1769480 | tf_op jit(solution)/shard_map/ppermute | solution.py:49
  149.9 4.6 %collective-permute-done.6 = bf16[192,1536]{1,0:T(8,128)(2,1)S(1)} collective-permute-done((bf16[192,1536]{1,0:T(8,128)(2,1)S(1)}, bf16[192,1536]{1,0:T(8,128)(2,1)S(1)}, u32[]{:S(2)}, u32[]{:S(2)}) %collective-permute-start.6) | collective-permute-done | bytes 589856 | tf_op jit(solution)/shard_map/ppermute | solution.py:49
  162.3 2.5 fusion
  169.2 2.5 fusion.1
  171.7 3.9 %collective-permute-start.16 = (bf16[128,1536]{1,0:T(8,128)(2,1)S(1)}, bf16[128,1536]{1,0:T(8,128)(2,1)S(1)}, u32[]{:S(2)}, u32[]{:S(2)}) collective-permute-start(bf16[128,1536]{1,0:T(8,128)(2,1)S(1)} %slice.125), channel_id=1, source_target_pairs={{0,1},{1,0},{2,3},{3,2},{4,5},{5,4},{6,7},{7,6},{8,9},{9,8},{10,11... | collective-permute-start | bytes 1179656 | tf_op jit(solution)/shard_map/ppermute | solution.py:28
  175.7 3.0 collective-permute-done.11
  180.7 7.9 %collective-permute-done.16 = bf16[128,1536]{1,0:T(8,128)(2,1)S(1)} collective-permute-done((bf16[128,1536]{1,0:T(8,128)(2,1)S(1)}, bf16[128,1536]{1,0:T(8,128)(2,1)S(1)}, u32[]{:S(2)}, u32[]{:S(2)}) %collective-permute-start.16) | collective-permute-done | bytes 393248 | tf_op jit(solution)/shard_map/ppermute | solution.py:28
  188.7 2.7 collective-permute-start.17
  191.9 10.3 %collective-permute-done.17 = bf16[64,1536]{1,0:T(8,128)(2,1)S(1)} collective-permute-done((bf16[64,1536]{1,0:T(8,128)(2,1)S(1)}, bf16[64,1536]{1,0:T(8,128)(2,1)S(1)}, u32[]{:S(2)}, u32[]{:S(2)}) %collective-permute-start.17) | collective-permute-done | bytes 196640 | tf_op jit(solution)/shard_map/ppermute | solution.py:28
  204.5 4.8 %collective-permute-start.18 = (bf16[64,1536]{1,0:T(8,128)(2,1)S(1)}, bf16[64,1536]{1,0:T(8,128)(2,1)S(1)}, u32[]{:S(2)}, u32[]{:S(2)}) collective-permute-start(bf16[64,1536]{1,0:T(8,128)(2,1)S(1)} %get-tuple-element.17), channel_id=1, source_target_pairs={{0,2},{2,0},{1,3},{3,1},{4,6},{6,4},{5,7},{7,5},{8,10},{10,8},{9,1... | collective-permute-start | bytes 589832 | tf_op jit(solution)/shard_map/ppermute | solution.py:28
  209.4 10.4 %collective-permute-done.13 = bf16[64,1536]{1,0:T(8,128)(2,1)S(1)} collective-permute-done((bf16[64,1536]{1,0:T(8,128)(2,1)S(1)}, bf16[64,1536]{1,0:T(8,128)(2,1)S(1)}, u32[]{:S(2)}, u32[]{:S(2)}) %collective-permute-start.13) | collective-permute-done | bytes 196640 | tf_op jit(solution)/shard_map/ppermute | solution.py:28
  225.9 7.8 %collective-permute-done.14 = bf16[128,1536]{1,0:T(8,128)(2,1)S(1)} collective-permute-done((bf16[128,1536]{1,0:T(8,128)(2,1)S(1)}, bf16[128,1536]{1,0:T(8,128)(2,1)S(1)}, u32[]{:S(2)}, u32[]{:S(2)}) %collective-permute-start.14) | collective-permute-done | bytes 393248 | tf_op jit(solution)/shard_map/ppermute | solution.py:28
  233.7 2.5 convolution_convert_fusion.2
  236.2 2.5 convolution_convert_fusion.3
  241.1 2.5 convolution_convert_fusion
  243.5 2.5 convolution_convert_fusion.1
  247.7 22.4 %all_to_all.15 = bf16[4,768,256]{2,1,0:T(8,128)(2,1)S(1)} all-to-all(bf16[4,768,256]{2,1,0:T(8,128)(2,1)S(1)} %bitcast.74), channel_id=1, replica_groups=mesh['zh'=2,'y'=4,'x'=4,'core'=2,'z4'=2,'z2'=2,'z1'=2] {'y'}, dimensions={0} | all-to-all | bytes 3145728 | tf_op jit(solution)/shard_map/all_to_all | solution.py:101
  270.4 4.4 %collective-permute-start.20 = (bf16[2,2,96,256]{3,2,1,0:T(8,128)(2,1)S(1)}, bf16[2,2,96,256]{3,2,1,0:T(8,128)(2,1)S(1)}, u32[]{:S(2)}, u32[]{:S(2)}) collective-permute-start(bf16[2,2,96,256]{3,2,1,0:T(8,128)(2,1)S(1)} %bitcast.98), channel_id=1, source_target_pairs={{0,4},{4,0},{1,5},{5,1},{2,6},{6,2},{3,7},{7,3},{8,12},{12,8},{9,1... | collective-permute-start | bytes 589832 | tf_op jit(solution)/shard_map/ppermute | solution.py:28
  274.8 19.8 %collective-permute-done.20 = bf16[2,2,96,256]{3,2,1,0:T(8,128)(2,1)S(1)} collective-permute-done((bf16[2,2,96,256]{3,2,1,0:T(8,128)(2,1)S(1)}, bf16[2,2,96,256]{3,2,1,0:T(8,128)(2,1)S(1)}, u32[]{:S(2)}, u32[]{:S(2)}) %collective-permute-start.20) | collective-permute-done | bytes 196640 | tf_op jit(solution)/shard_map/ppermute | solution.py:28
  294.7 3.2 %collective-permute-start.21 = (bf16[2,96,256]{2,1,0:T(8,128)(2,1)S(1)}, bf16[2,96,256]{2,1,0:T(8,128)(2,1)S(1)}, u32[]{:S(2)}, u32[]{:S(2)}) collective-permute-start(bf16[2,96,256]{2,1,0:T(8,128)(2,1)S(1)} %fusion.12), channel_id=1, source_target_pairs={{0,256},{256,0},{1,257},{257,1},{2,258},{258,2},{3,259},{259,3},{4... | collective-permute-start | bytes 294920 | tf_op jit(solution)/shard_map/ppermute | solution.py:28
  297.9 12.0 %collective-permute-done.21 = bf16[2,96,256]{2,1,0:T(8,128)(2,1)S(1)} collective-permute-done((bf16[2,96,256]{2,1,0:T(8,128)(2,1)S(1)}, bf16[2,96,256]{2,1,0:T(8,128)(2,1)S(1)}, u32[]{:S(2)}, u32[]{:S(2)}) %collective-permute-start.21) | collective-permute-done | bytes 98336 | tf_op jit(solution)/shard_map/ppermute | solution.py:28
  (83 shorter events, 52.2 us)
Async XLA Ops:
  0.6 34.3 %copy-start = (bf16[3072,96]{0,1:T(8,128)(2,1)S(1)}, bf16[3072,96]{0,1:T(8,128)(2,1)}, u32[]{:S(2)}) copy-start(bf16[3072,96]{0,1:T(8,128)(2,1)} %param.6) | copy-start | bytes 1769476
  2.7 21.1 %collective-permute-start = (bf16[192,256]{0,1:T(8,128)(2,1)S(1)}, bf16[192,256]{0,1:T(8,128)(2,1)S(1)}, u32[]{:S(2)}, u32[]{:S(2)}) collective-permute-start(bf16[192,256]{0,1:T(8,128)(2,1)S(1)} %bitcast.87), channel_id=1, source_target_pairs={{0,256},{256,0},{1,257},{257,1},{2,258},{258,2},{3,259},{259,3},{4... | collective-permute-start | bytes 294920 | tf_op jit(solution)/shard_map/ppermute | solution.py:28
  19.6 78.2 %collective-permute-start.2 = (bf16[96,1536]{1,0:T(8,128)(2,1)S(1)}, bf16[96,1536]{1,0:T(8,128)(2,1)S(1)}, u32[]{:S(2)}, u32[]{:S(2)}) collective-permute-start(bf16[96,1536]{1,0:T(8,128)(2,1)S(1)} %get-tuple-element.25), channel_id=1, source_target_pairs={{0,4},{4,0},{1,5},{5,1},{2,6},{6,2},{3,7},{7,3},{8,12},{12,8},{9,1... | collective-permute-start | bytes 884744 | tf_op jit(solution)/shard_map/ppermute | solution.py:28
  23.9 73.7 %collective-permute-start.1 = (bf16[2,192,256]{1,2,0:T(8,128)(2,1)S(1)}, bf16[2,192,256]{1,2,0:T(8,128)(2,1)S(1)}, u32[]{:S(2)}, u32[]{:S(2)}) collective-permute-start(bf16[2,192,256]{1,2,0:T(8,128)(2,1)S(1)} %get-tuple-element.27), channel_id=1, source_target_pairs={{0,4},{4,0},{1,5},{5,1},{2,6},{6,2},{3,7},{7,3},{8,12},{12,8},{9,1... | collective-permute-start | bytes 589832 | tf_op jit(solution)/shard_map/ppermute | solution.py:28
  35.0 68.9 %collective-permute-start.3 = (bf16[96,1536]{1,0:T(8,128)(2,1)S(1)}, bf16[96,1536]{1,0:T(8,128)(2,1)S(1)}, u32[]{:S(2)}, u32[]{:S(2)}) collective-permute-start(bf16[96,1536]{1,0:T(8,128)(2,1)S(1)} %get-tuple-element.23), channel_id=1, source_target_pairs={{0,4},{4,0},{1,5},{5,1},{2,6},{6,2},{3,7},{7,3},{8,12},{12,8},{9,1... | collective-permute-start | bytes 884744 | tf_op jit(solution)/shard_map/ppermute | solution.py:28
  103.9 19.3 %collective-permute-start.8 = (bf16[192,1536]{1,0:T(8,128)(2,1)S(1)}, bf16[192,1536]{1,0:T(8,128)(2,1)S(1)}, u32[]{:S(2)}, u32[]{:S(2)}) collective-permute-start(bf16[192,1536]{1,0:T(8,128)(2,1)S(1)} %pad_maximum_fusion.3), channel_id=1, source_target_pairs={{0,48},{16,32},{32,16},{48,0},{1,49},{17,33},{33,17},{49,1},{2,50}... | collective-permute-start | bytes 1769480 | tf_op jit(solution)/shard_map/ppermute | solution.py:43
  108.6 18.2 %collective-permute-start.7 = (bf16[192,1536]{1,0:T(8,128)(2,1)S(1)}, bf16[192,1536]{1,0:T(8,128)(2,1)}, u32[]{:S(2)}, u32[]{:S(2)}) collective-permute-start(bf16[192,1536]{1,0:T(8,128)(2,1)S(1)} %pad_maximum_fusion.3), channel_id=1, source_target_pairs={{0,16},{16,0},{32,48},{48,32},{1,17},{17,1},{33,49},{49,33},{2,18}... | collective-permute-start | bytes 1769480 | tf_op jit(solution)/shard_map/ppermute | solution.py:43
  110.8 27.7 %collective-permute-start.5 = (bf16[192,1536]{1,0:T(8,128)(2,1)S(1)}, bf16[192,1536]{1,0:T(8,128)(2,1)S(1)}, u32[]{:S(2)}, u32[]{:S(2)}) collective-permute-start(bf16[192,1536]{1,0:T(8,128)(2,1)S(1)} %pad_maximum_fusion.4), channel_id=1, source_target_pairs={{0,48},{16,32},{32,16},{48,0},{1,49},{17,33},{33,17},{49,1},{2,50}... | collective-permute-start | bytes 1769480 | tf_op jit(solution)/shard_map/ppermute | solution.py:43
  113.8 25.7 %collective-permute-start.4 = (bf16[192,1536]{1,0:T(8,128)(2,1)S(1)}, bf16[192,1536]{1,0:T(8,128)(2,1)}, u32[]{:S(2)}, u32[]{:S(2)}) collective-permute-start(bf16[192,1536]{1,0:T(8,128)(2,1)S(1)} %pad_maximum_fusion.4), channel_id=1, source_target_pairs={{0,16},{16,0},{32,48},{48,32},{1,17},{17,1},{33,49},{49,33},{2,18}... | collective-permute-start | bytes 1769480 | tf_op jit(solution)/shard_map/ppermute | solution.py:43
  129.1 16.1 %collective-permute-start.9 = (bf16[192,1536]{1,0:T(8,128)(2,1)}, bf16[192,1536]{1,0:T(8,128)(2,1)}, u32[]{:S(2)}, u32[]{:S(2)}) collective-permute-start(bf16[192,1536]{1,0:T(8,128)(2,1)} %get-tuple-element.20), channel_id=1, source_target_pairs={{0,48},{8,24},{16,32},{24,8},{32,16},{40,56},{48,0},{56,40},{1,49}... | collective-permute-start | bytes 1769480 | tf_op jit(solution)/shard_map/ppermute | solution.py:49
  133.8 24.4 %all-to-all-start = ((bf16[4,768,256]{2,1,0:T(8,128)(2,1)}), bf16[4,768,256]{2,1,0:T(8,128)(2,1)S(1)}, u32[]{:S(2)}, u32[]{:S(2)}) async-start(bf16[4,768,256]{2,1,0:T(8,128)(2,1)} %broadcast_in_dim.8), calls=%async_computation | async-start | bytes 3145728 | tf_op jit(solution)/shard_map/all_to_all | solution.py:71
  141.5 13.0 %collective-permute-start.6 = (bf16[192,1536]{1,0:T(8,128)(2,1)S(1)}, bf16[192,1536]{1,0:T(8,128)(2,1)S(1)}, u32[]{:S(2)}, u32[]{:S(2)}) collective-permute-start(bf16[192,1536]{1,0:T(8,128)(2,1)S(1)} %get-tuple-element.18), channel_id=1, source_target_pairs={{0,48},{8,24},{16,32},{24,8},{32,16},{40,56},{48,0},{56,40},{1,49}... | collective-permute-start | bytes 1769480 | tf_op jit(solution)/shard_map/ppermute | solution.py:49
  148.0 11.9 %collective-permute-start.10 = (bf16[768,1536]{1,0:T(8,128)(2,1)}, bf16[768,1536]{1,0:T(8,128)(2,1)}, u32[]{:S(2)}, u32[]{:S(2)}) collective-permute-start(bf16[768,1536]{1,0:T(8,128)(2,1)} %constant_dynamic-update-slice_fusion.4), channel_id=1, source_target_pairs={{0,8},{8,0},{1,9},{9,1},{2,10},{10,2},{3,11},{11,3},{4,12},{12,4},... | collective-permute-start | bytes 7077896 | tf_op jit(solution)/shard_map/ppermute | solution.py:28
  156.2 10.6 %collective-permute-start.15 = (bf16[768,1536]{1,0:T(8,128)(2,1)}, bf16[768,1536]{1,0:T(8,128)(2,1)}, u32[]{:S(2)}, u32[]{:S(2)}) collective-permute-start(bf16[768,1536]{1,0:T(8,128)(2,1)} %constant_dynamic-update-slice_fusion), channel_id=1, source_target_pairs={{0,8},{8,0},{1,9},{9,1},{2,10},{10,2},{3,11},{11,3},{4,12},{12,4},... | collective-permute-start | bytes 7077896 | tf_op jit(solution)/shard_map/ppermute | solution.py:28
  164.8 13.8 %collective-permute-start.11 = (bf16[128,1536]{1,0:T(8,128)(2,1)S(1)}, bf16[128,1536]{1,0:T(8,128)(2,1)S(1)}, u32[]{:S(2)}, u32[]{:S(2)}) collective-permute-start(bf16[128,1536]{1,0:T(8,128)(2,1)S(1)} %slice.119), channel_id=1, source_target_pairs={{0,1},{1,0},{2,3},{3,2},{4,5},{5,4},{6,7},{7,6},{8,9},{9,8},{10,11... | collective-permute-start | bytes 1179656 | tf_op jit(solution)/shard_map/ppermute | solution.py:28
  171.7 16.9 %collective-permute-start.16 = (bf16[128,1536]{1,0:T(8,128)(2,1)S(1)}, bf16[128,1536]{1,0:T(8,128)(2,1)S(1)}, u32[]{:S(2)}, u32[]{:S(2)}) collective-permute-start(bf16[128,1536]{1,0:T(8,128)(2,1)S(1)} %slice.125), channel_id=1, source_target_pairs={{0,1},{1,0},{2,3},{3,2},{4,5},{5,4},{6,7},{7,6},{8,9},{9,8},{10,11... | collective-permute-start | bytes 1179656 | tf_op jit(solution)/shard_map/ppermute | solution.py:28
  178.8 13.2 %collective-permute-start.12 = (bf16[64,1536]{1,0:T(8,128)(2,1)S(1)}, bf16[64,1536]{1,0:T(8,128)(2,1)S(1)}, u32[]{:S(2)}, u32[]{:S(2)}) collective-permute-start(bf16[64,1536]{1,0:T(8,128)(2,1)S(1)} %slice.121), channel_id=1, source_target_pairs={{0,2},{2,0},{1,3},{3,1},{4,6},{6,4},{5,7},{7,5},{8,10},{10,8},{9,1... | collective-permute-start | bytes 589832 | tf_op jit(solution)/shard_map/ppermute | solution.py:28
  188.7 13.5 %collective-permute-start.17 = (bf16[64,1536]{1,0:T(8,128)(2,1)S(1)}, bf16[64,1536]{1,0:T(8,128)(2,1)S(1)}, u32[]{:S(2)}, u32[]{:S(2)}) collective-permute-start(bf16[64,1536]{1,0:T(8,128)(2,1)S(1)} %slice.127), channel_id=1, source_target_pairs={{0,2},{2,0},{1,3},{3,1},{4,6},{6,4},{5,7},{7,5},{8,10},{10,8},{9,1... | collective-permute-start | bytes 589832 | tf_op jit(solution)/shard_map/ppermute | solution.py:28
  202.6 17.2 %collective-permute-start.13 = (bf16[64,1536]{1,0:T(8,128)(2,1)S(1)}, bf16[64,1536]{1,0:T(8,128)(2,1)S(1)}, u32[]{:S(2)}, u32[]{:S(2)}) collective-permute-start(bf16[64,1536]{1,0:T(8,128)(2,1)S(1)} %get-tuple-element.16), channel_id=1, source_target_pairs={{0,2},{2,0},{1,3},{3,1},{4,6},{6,4},{5,7},{7,5},{8,10},{10,8},{9,1... | collective-permute-start | bytes 589832 | tf_op jit(solution)/shard_map/ppermute | solution.py:28
  204.5 19.4 %collective-permute-start.18 = (bf16[64,1536]{1,0:T(8,128)(2,1)S(1)}, bf16[64,1536]{1,0:T(8,128)(2,1)S(1)}, u32[]{:S(2)}, u32[]{:S(2)}) collective-permute-start(bf16[64,1536]{1,0:T(8,128)(2,1)S(1)} %get-tuple-element.17), channel_id=1, source_target_pairs={{0,2},{2,0},{1,3},{3,1},{4,6},{6,4},{5,7},{7,5},{8,10},{10,8},{9,1... | collective-permute-start | bytes 589832 | tf_op jit(solution)/shard_map/ppermute | solution.py:28
  219.8 13.9 %collective-permute-start.14 = (bf16[128,1536]{1,0:T(8,128)(2,1)S(1)}, bf16[128,1536]{1,0:T(8,128)(2,1)S(1)}, u32[]{:S(2)}, u32[]{:S(2)}) collective-permute-start(bf16[128,1536]{1,0:T(8,128)(2,1)S(1)} %pad_maximum_fusion.6), channel_id=1, source_target_pairs={{0,1},{1,0},{2,3},{3,2},{4,5},{5,4},{6,7},{7,6},{8,9},{9,8},{10,11... | collective-permute-start | bytes 1179656 | tf_op jit(solution)/shard_map/ppermute | solution.py:28
  223.9 17.1 %collective-permute-start.19 = (bf16[128,1536]{1,0:T(8,128)(2,1)S(1)}, bf16[128,1536]{1,0:T(8,128)(2,1)S(1)}, u32[]{:S(2)}, u32[]{:S(2)}) collective-permute-start(bf16[128,1536]{1,0:T(8,128)(2,1)S(1)} %pad_maximum_fusion.7), channel_id=1, source_target_pairs={{0,1},{1,0},{2,3},{3,2},{4,5},{5,4},{6,7},{7,6},{8,9},{9,8},{10,11... | collective-permute-start | bytes 1179656 | tf_op jit(solution)/shard_map/ppermute | solution.py:28
  270.4 24.2 %collective-permute-start.20 = (bf16[2,2,96,256]{3,2,1,0:T(8,128)(2,1)S(1)}, bf16[2,2,96,256]{3,2,1,0:T(8,128)(2,1)S(1)}, u32[]{:S(2)}, u32[]{:S(2)}) collective-permute-start(bf16[2,2,96,256]{3,2,1,0:T(8,128)(2,1)S(1)} %bitcast.98), channel_id=1, source_target_pairs={{0,4},{4,0},{1,5},{5,1},{2,6},{6,2},{3,7},{7,3},{8,12},{12,8},{9,1... | collective-permute-start | bytes 589832 | tf_op jit(solution)/shard_map/ppermute | solution.py:28
  294.7 15.2 %collective-permute-start.21 = (bf16[2,96,256]{2,1,0:T(8,128)(2,1)S(1)}, bf16[2,96,256]{2,1,0:T(8,128)(2,1)S(1)}, u32[]{:S(2)}, u32[]{:S(2)}) collective-permute-start(bf16[2,96,256]{2,1,0:T(8,128)(2,1)S(1)} %fusion.12), channel_id=1, source_target_pairs={{0,256},{256,0},{1,257},{257,1},{2,258},{258,2},{3,259},{259,3},{4... | collective-permute-start | bytes 294920 | tf_op jit(solution)/shard_map/ppermute | solution.py:28

commit v4 on v2

--- a/solution.py
+++ b/solution.py
@@ -34,9 +34,9 @@
 
 def half_swapped(weights):
     low, high = weights[:, :, :1536], weights[:, :, 1536:]
-    bit = lax.axis_index("z1") == 1
+    bit = lax.axis_index("z2") == 1
     kept, sent = jnp.where(bit, high, low), jnp.where(bit, low, high)
-    return jnp.stack([kept, swap(sent, "z1")], 1)
+    return jnp.stack([kept, swap(sent, "z2")], 1)
 
 
 def neighbours(block):
@@ -53,21 +53,17 @@
 def own_order(columns):
     blocks = columns.reshape(columns.shape[:-1] + (2, 2, 64))
     axis = blocks.ndim - 3
-    blocks = flip_if(blocks, lax.axis_index("z2"), axis)
+    blocks = flip_if(blocks, lax.axis_index("z1"), axis)
     blocks = flip_if(blocks, lax.axis_index("z4"), axis + 1)
     return blocks.reshape(columns.shape)
 
 
-def over_zh(shards):
-    return jnp.stack([shards, swap(shards, "zh")])
-
-
 def gathered_rows(both):
-    sent = jnp.broadcast_to(both[None], (8, 2, 192, 256))
-    rows = lax.all_to_all(sent, ("y", "z1"), 0, 0, tiled=True)
+    quad = jnp.concatenate([both, swap(both, "z2")], 0)
+    sent = jnp.broadcast_to(quad[None], (4, 768, 256)).reshape(3072, 256)
+    rows = lax.all_to_all(sent, "y", 0, 0, tiled=True)
     rows = rows.reshape(4, 2, 2, 2, 96, 256).transpose(3, 2, 0, 1, 4, 5)
-    rows = flip_if(rows, lax.axis_index("zh"), 1)
-    return flip_if(rows, lax.axis_index("z1"), 3)
+    return flip_if(rows, lax.axis_index("zh"), 1)
 
 
 def core_x_order(blocks):
@@ -79,7 +75,7 @@
 
 def spread_sum(partial_value):
     total = partial_value
-    for name in ("z2", "z4"):
+    for name in ("z1", "z4"):
         half = total.shape[0] // 2
         sent = total[half:].astype(jnp.bfloat16)
         total = total[:half].astype(jnp.bfloat16).astype(jnp.float32) + swap(sent, name).astype(jnp.float32)
@@ -87,17 +83,19 @@
 
 
 def all_tokens(rows):
-    for name in ("z4", "z2"):
+    for name in ("z4", "z1"):
         rows = jnp.concatenate([rows, swap(rows, name)], 0)
     return rows
 
 
-def over_y(blocks):
+def over_gx(blocks):
     blocks = flip_if(blocks, lax.axis_index("zh"), 1)
-    blocks = flip_if(blocks, lax.axis_index("z1"), 3)
-    sent = blocks.transpose(2, 3, 0, 1, 4, 5).reshape(8, 2, 2, 96, 256)
-    parts = lax.all_to_all(sent, ("y", "z1"), 0, 0, tiled=True)
-    return parts.astype(jnp.float32).sum(0)
+    sent = blocks.transpose(2, 3, 1, 0, 4, 5).reshape(3072, 256)
+    parts = lax.all_to_all(sent, "y", 0, 0, tiled=True)
+    total = parts.reshape(4, 2, 2, 2, 96, 256).astype(jnp.float32).sum(0)
+    total = total[0] + swap(total[1].astype(jnp.bfloat16), "z2").astype(jnp.float32)
+    total = total[0] + swap(total[1].astype(jnp.bfloat16), "zh").astype(jnp.float32)
+    return total.astype(jnp.bfloat16)
 
 
 def contract(left, right, dims):
@@ -118,7 +116,7 @@
     shards = own_order(jnp.concatenate([tokens.T, grad_output.T], 0))
     halves = half_swapped(jnp.stack([up_weight, down_weight.T]))
     shards, halves = lax.optimization_barrier((shards, halves))
-    both = over_zh(shards)
+    both = jnp.concatenate([shards, swap(shards, "zh")], 0)
     one, three = neighbours(halves)
     both, one, three = lax.optimization_barrier((both, one, three))
     rows = gathered_rows(both)
@@ -127,14 +125,12 @@
     rows = core_x_order(rows.reshape(2, 2, 2, 2, 192, 256).transpose(1, 2, 3, 0, 4, 5))
     rows = rows.transpose(3, 2, 0, 1, 4, 5).reshape(2, 2, 768, 256)
     hidden = spread_sum(product(rows[0], up_own, up_other))
+    grad_act = spread_sum(product(rows[1], down_own, down_other))
     activated = all_tokens(gelu_value(hidden).astype(jnp.bfloat16))
-    grad_act = spread_sum(product(rows[1], down_own, down_other))
     grad_hidden = all_tokens((grad_act * gelu_slope(hidden)).astype(jnp.bfloat16))
     output = back_product(down_own, down_other, activated)
     grad_tokens = back_product(up_own, up_other, grad_hidden)
-    sums = over_y(jnp.stack([output, grad_tokens]))
-    other = swap(sums[:, 1].astype(jnp.bfloat16), "zh")
-    both = own_order((sums[:, 0] + other.astype(jnp.float32)).astype(jnp.bfloat16))
+    both = own_order(over_gx(jnp.stack([output, grad_tokens])))
     return (both[0].T, both[1].T)
 
 

time: 294 us -> 284 us (0.966)
  the two profiles are of different devices: /device:TPU:24 before, /device:TPU:34 now
where the time goes in v4:
time: 284 us; the launch traced here: 283 us
  starting transfers between devices  144 us (51%)
  waiting for transfers between devices  80.5 us (28%)
  blocking collectives  18.3 us (6%)
  matrix products  16.4 us (6%)
  other arithmetic  13.8 us (5%)
  local copies, waits for them, and re-layouts  8.66 us (3%)
    ppermute x15, starting transfers between devices, swap(): return lax.ppermute(array, axis, SWAP)  130 us
    ppermute x15, waiting for transfers between devices, swap(): return lax.ppermute(array, axis, SWAP)  63.6 us
    all_to_all x1, blocking collectives, over_gx(): parts = lax.all_to_all(sent, 'y', 0, 0, tiled=True)  18.3 us
    dot_general x8, matrix products, contract(): lax.dot_general(left, right, (dims, ((), ())), preferred_element_type=jnp...  16.4 us
    all_to_all x1, waiting for transfers between devices, gathered_rows(): rows = lax.all_to_all(sent, 'y', 0, 0, tiled=True)  10.5 us
    ppermute x2, starting transfers between devices, neighbours(): lax.ppermute(block, 'x', [(i, i ^ k) for i in range(4)])  7.11 us
    ppermute x2, waiting for transfers between devices, neighbours(): lax.ppermute(block, 'x', [(i, i ^ k) for i in range(4)])  6.42 us
  transfers between devices with their start and end apart: 19, of which 13 were waited for; matrix products, arithmetic and copies ran while one was open for 10% of the time, Pallas kernels for 0%

profile of v4, /device:TPU:34, one launch (start us, length us, event | category | flops | bytes accessed | tf_op | source)
XLA Modules:
  0.0 282.7 jit_solution(587783027364249449)
XLA Ops:
  2.3 5.2 %collective-permute-start = (bf16[2,96,1536]{2,1,0:T(8,128)(2,1)S(1)}, bf16[2,96,1536]{2,1,0:T(8,128)(2,1)S(1)}, u32[]{:S(2)}, u32[]{:S(2)}) collective-permute-start(bf16[2,96,1536]{2,1,0:T(8,128)(2,1)S(1)} %get-tuple-element.29), channel_id=1, source_target_pairs={{0,2},{2,0},{1,3},{3,1},{4,6},{6,4},{5,7},{7,5},{8,10},{10,8},{9,1... | collective-permute-start | bytes 1769480 | tf_op jit(solution)/shard_map/ppermute | solution.py:28
  8.6 23.7 %collective-permute-done = bf16[2,96,1536]{2,1,0:T(8,128)(2,1)S(1)} collective-permute-done((bf16[2,96,1536]{2,1,0:T(8,128)(2,1)S(1)}, bf16[2,96,1536]{2,1,0:T(8,128)(2,1)S(1)}, u32[]{:S(2)}, u32[]{:S(2)}) %collective-permute-start) | collective-permute-done | bytes 589856 | tf_op jit(solution)/shard_map/ppermute | solution.py:28
  32.4 3.4 %collective-permute-start.3 = (bf16[2,2,96,1536]{3,2,0,1:T(8,128)(2,1)S(1)}, bf16[2,2,96,1536]{3,2,0,1:T(8,128)(2,1)S(1)}, u32[]{:S(2)}, u32[]{:S(2)}) collective-permute-start(bf16[2,2,96,1536]{3,2,0,1:T(8,128)(2,1)S(1)} %pad_maximum_fusion.3), channel_id=1, source_target_pairs={{0,48},{16,32},{32,16},{48,0},{1,49},{17,33},{33,17},{49,1},{2,50}... | collective-permute-start | bytes 3538952 | tf_op jit(solution)/shard_map/ppermute | solution.py:43
  35.8 3.7 %collective-permute-start.2 = (bf16[2,2,96,1536]{3,2,0,1:T(8,128)(2,1)S(1)}, bf16[2,2,96,1536]{3,2,0,1:T(8,128)(2,1)S(1)}, u32[]{:S(2)}, u32[]{:S(2)}) collective-permute-start(bf16[2,2,96,1536]{3,2,0,1:T(8,128)(2,1)S(1)} %pad_maximum_fusion.3), channel_id=1, source_target_pairs={{0,16},{16,0},{32,48},{48,32},{1,17},{17,1},{33,49},{49,33},{2,18}... | collective-permute-start | bytes 3538952 | tf_op jit(solution)/shard_map/ppermute | solution.py:43
  39.5 13.5 %collective-permute-start.1 = (bf16[192,256]{0,1:T(8,128)(2,1)}, bf16[192,256]{0,1:T(8,128)(2,1)}, u32[]{:S(2)}, u32[]{:S(2)}) collective-permute-start(bf16[192,256]{0,1:T(8,128)(2,1)} %bitcast.3), channel_id=1, source_target_pairs={{0,256},{256,0},{1,257},{257,1},{2,258},{258,2},{3,259},{259,3},{4... | collective-permute-start | bytes 294920 | tf_op jit(solution)/shard_map/ppermute | solution.py:28
  53.0 4.9 %collective-permute-done.1 = bf16[192,256]{0,1:T(8,128)(2,1)} collective-permute-done((bf16[192,256]{0,1:T(8,128)(2,1)}, bf16[192,256]{0,1:T(8,128)(2,1)}, u32[]{:S(2)}, u32[]{:S(2)}) %collective-permute-start.1) | collective-permute-done | bytes 98336 | tf_op jit(solution)/shard_map/ppermute | solution.py:28
  59.0 3.2 %collective-permute-done.3 = bf16[2,2,96,1536]{3,2,0,1:T(8,128)(2,1)S(1)} collective-permute-done((bf16[2,2,96,1536]{3,2,0,1:T(8,128)(2,1)S(1)}, bf16[2,2,96,1536]{3,2,0,1:T(8,128)(2,1)S(1)}, u32[]{:S(2)}, u32[]{:S(2)}) %collective-permute-start.3) | collective-permute-done | bytes 1179680 | tf_op jit(solution)/shard_map/ppermute | solution.py:43
  62.2 3.2 %collective-permute-done.2 = bf16[2,2,96,1536]{3,2,0,1:T(8,128)(2,1)S(1)} collective-permute-done((bf16[2,2,96,1536]{3,2,0,1:T(8,128)(2,1)S(1)}, bf16[2,2,96,1536]{3,2,0,1:T(8,128)(2,1)S(1)}, u32[]{:S(2)}, u32[]{:S(2)}) %collective-permute-start.2) | collective-permute-done | bytes 1179680 | tf_op jit(solution)/shard_map/ppermute | solution.py:43
  70.0 5.3 %collective-permute-start.5 = (bf16[384,256]{0,1:T(8,128)(2,1)S(1)}, bf16[384,256]{0,1:T(8,128)(2,1)S(1)}, u32[]{:S(2)}, u32[]{:S(2)}) collective-permute-start(bf16[384,256]{0,1:T(8,128)(2,1)S(1)} %pad_maximum_fusion.14), channel_id=1, source_target_pairs={{0,2},{2,0},{1,3},{3,1},{4,6},{6,4},{5,7},{7,5},{8,10},{10,8},{9,1... | collective-permute-start | bytes 589832 | tf_op jit(solution)/shard_map/ppermute | solution.py:28
  76.8 3.5 %collective-permute-done.5 = bf16[384,256]{0,1:T(8,128)(2,1)S(1)} collective-permute-done((bf16[384,256]{0,1:T(8,128)(2,1)S(1)}, bf16[384,256]{0,1:T(8,128)(2,1)S(1)}, u32[]{:S(2)}, u32[]{:S(2)}) %collective-permute-start.5) | collective-permute-done | bytes 196640 | tf_op jit(solution)/shard_map/ppermute | solution.py:28
  81.8 4.5 %all-to-all-start = ((bf16[4,768,256]{2,1,0:T(8,128)(2,1)}), bf16[4,768,256]{2,1,0:T(8,128)(2,1)}, u32[]{:S(2)}, u32[]{:S(2)}) async-start(bf16[4,768,256]{2,1,0:T(8,128)(2,1)} %broadcast_in_dim.2), calls=%async_computation | async-start | bytes 3145728 | tf_op jit(solution)/shard_map/all_to_all | solution.py:64
  90.8 2.8 %pad_maximum_fusion = bf16[768,1536]{1,0:T(8,128)(2,1)} fusion(bf16[192,1536]{1,0:T(8,128)(2,1)S(1)} %bitcast.86, bf16[192,1536]{1,0:T(8,128)(2,1)} %bitcast.90, bf16[192,1536]{1,0:T(8,128)(2,1)S(1)} %bitcast.85, bf16[192,1536]{1,0:T(8,128)(2,1)} %bitcast.89), kind=kLoop, calls=%fused_computation.10 | loop fusion | flops 9437184 | bytes 4718592 | tf_op jit(solution)/shard_map/concatenate | solution.py:50
  96.1 10.5 %all-to-all-done = bf16[4,768,256]{2,1,0:T(8,128)(2,1)} async-done(((bf16[4,768,256]{2,1,0:T(8,128)(2,1)}), bf16[4,768,256]{2,1,0:T(8,128)(2,1)}, u32[]{:S(2)}, u32[]{:S(2)}) %all-to-all-start) | async-done | bytes 1572896 | tf_op jit(solution)/shard_map/all_to_all | solution.py:64
  106.6 2.5 reverse_select_fusion.4
  111.2 2.5 fusion
  120.6 3.9 %collective-permute-start.12 = (bf16[128,1536]{1,0:T(8,128)(2,1)S(1)}, bf16[128,1536]{1,0:T(8,128)(2,1)S(1)}, u32[]{:S(2)}, u32[]{:S(2)}) collective-permute-start(bf16[128,1536]{1,0:T(8,128)(2,1)S(1)} %slice.151), channel_id=1, source_target_pairs={{0,1},{1,0},{2,3},{3,2},{4,5},{5,4},{6,7},{7,6},{8,9},{9,8},{10,11... | collective-permute-start | bytes 1179656 | tf_op jit(solution)/shard_map/ppermute | solution.py:28
  126.3 9.1 %collective-permute-start.8 = (bf16[64,1536]{1,0:T(8,128)(2,1)S(1)}, bf16[64,1536]{1,0:T(8,128)(2,1)S(1)}, u32[]{:S(2)}, u32[]{:S(2)}) collective-permute-start(bf16[64,1536]{1,0:T(8,128)(2,1)S(1)} %slice.147), channel_id=1, source_target_pairs={{0,4},{4,0},{1,5},{5,1},{2,6},{6,2},{3,7},{7,3},{8,12},{12,8},{9,1... | collective-permute-start | bytes 589832 | tf_op jit(solution)/shard_map/ppermute | solution.py:28
  135.6 20.4 %collective-permute-start.13 = (bf16[64,1536]{1,0:T(8,128)(2,1)S(1)}, bf16[64,1536]{1,0:T(8,128)(2,1)S(1)}, u32[]{:S(2)}, u32[]{:S(2)}) collective-permute-start(bf16[64,1536]{1,0:T(8,128)(2,1)S(1)} %slice.153), channel_id=1, source_target_pairs={{0,4},{4,0},{1,5},{5,1},{2,6},{6,2},{3,7},{7,3},{8,12},{12,8},{9,1... | collective-permute-start | bytes 589832 | tf_op jit(solution)/shard_map/ppermute | solution.py:28
  156.0 5.9 %collective-permute-done.8 = bf16[64,1536]{1,0:T(8,128)(2,1)S(1)} collective-permute-done((bf16[64,1536]{1,0:T(8,128)(2,1)S(1)}, bf16[64,1536]{1,0:T(8,128)(2,1)S(1)}, u32[]{:S(2)}, u32[]{:S(2)}) %collective-permute-start.8) | collective-permute-done | bytes 196640 | tf_op jit(solution)/shard_map/ppermute | solution.py:28
  161.8 5.4 %collective-permute-done.13 = bf16[64,1536]{1,0:T(8,128)(2,1)S(1)} collective-permute-done((bf16[64,1536]{1,0:T(8,128)(2,1)S(1)}, bf16[64,1536]{1,0:T(8,128)(2,1)S(1)}, u32[]{:S(2)}, u32[]{:S(2)}) %collective-permute-start.13) | collective-permute-done | bytes 196640 | tf_op jit(solution)/shard_map/ppermute | solution.py:28
  167.5 8.4 %collective-permute-start.9 = (bf16[64,1536]{1,0:T(8,128)(2,1)S(1)}, bf16[64,1536]{1,0:T(8,128)(2,1)S(1)}, u32[]{:S(2)}, u32[]{:S(2)}) collective-permute-start(bf16[64,1536]{1,0:T(8,128)(2,1)S(1)} %get-tuple-element.30), channel_id=1, source_target_pairs={{0,4},{4,0},{1,5},{5,1},{2,6},{6,2},{3,7},{7,3},{8,12},{12,8},{9,1... | collective-permute-start | bytes 589832 | tf_op jit(solution)/shard_map/ppermute | solution.py:28
  179.6 18.6 %collective-permute-start.10 = (bf16[128,1536]{1,0:T(8,128)(2,1)S(1)}, bf16[128,1536]{1,0:T(8,128)(2,1)S(1)}, u32[]{:S(2)}, u32[]{:S(2)}) collective-permute-start(bf16[128,1536]{1,0:T(8,128)(2,1)S(1)} %pad_maximum_fusion.8), channel_id=1, source_target_pairs={{0,1},{1,0},{2,3},{3,2},{4,5},{5,4},{6,7},{7,6},{8,9},{9,8},{10,11... | collective-permute-start | bytes 1179656 | tf_op jit(solution)/shard_map/ppermute | solution.py:28
  198.3 3.1 %collective-permute-start.15 = (bf16[128,1536]{1,0:T(8,128)(2,1)S(1)}, bf16[128,1536]{1,0:T(8,128)(2,1)S(1)}, u32[]{:S(2)}, u32[]{:S(2)}) collective-permute-start(bf16[128,1536]{1,0:T(8,128)(2,1)S(1)} %pad_maximum_fusion.9), channel_id=1, source_target_pairs={{0,1},{1,0},{2,3},{3,2},{4,5},{5,4},{6,7},{7,6},{8,9},{9,8},{10,11... | collective-permute-start | bytes 1179656 | tf_op jit(solution)/shard_map/ppermute | solution.py:28
  201.4 2.7 collective-permute-done.10
  204.1 2.5 convolution_convert_fusion.2
  206.6 2.5 convolution_convert_fusion.3
  209.6 2.5 convolution_convert_fusion
  214.1 18.3 %all_to_all.15 = bf16[4,768,256]{2,1,0:T(8,128)(2,1)S(1)} all-to-all(bf16[4,768,256]{2,1,0:T(8,128)(2,1)S(1)} %bitcast.81), channel_id=1, replica_groups=mesh['zh'=2,'y'=4,'x'=4,'core'=2,'z4'=2,'z2'=2,'z1'=2] {'y'}, dimensions={0} | all-to-all | bytes 3145728 | tf_op jit(solution)/shard_map/all_to_all | solution.py:94
  232.7 20.5 %collective-permute-start.16 = (bf16[2,2,96,256]{3,2,1,0:T(8,128)(2,1)S(1)}, bf16[2,2,96,256]{3,2,1,0:T(8,128)(2,1)S(1)}, u32[]{:S(2)}, u32[]{:S(2)}) collective-permute-start(bf16[2,2,96,256]{3,2,1,0:T(8,128)(2,1)S(1)} %bitcast.111), channel_id=1, source_target_pairs={{0,2},{2,0},{1,3},{3,1},{4,6},{6,4},{5,7},{7,5},{8,10},{10,8},{9,1... | collective-permute-start | bytes 589832 | tf_op jit(solution)/shard_map/ppermute | solution.py:28
  253.2 5.7 %collective-permute-done.16 = bf16[2,2,96,256]{3,2,1,0:T(8,128)(2,1)S(1)} collective-permute-done((bf16[2,2,96,256]{3,2,1,0:T(8,128)(2,1)S(1)}, bf16[2,2,96,256]{3,2,1,0:T(8,128)(2,1)S(1)}, u32[]{:S(2)}, u32[]{:S(2)}) %collective-permute-start.16) | collective-permute-done | bytes 196640 | tf_op jit(solution)/shard_map/ppermute | solution.py:28
  259.0 13.5 %collective-permute-start.17 = (bf16[2,96,256]{2,1,0:T(8,128)(2,1)S(1)}, bf16[2,96,256]{2,1,0:T(8,128)(2,1)S(1)}, u32[]{:S(2)}, u32[]{:S(2)}) collective-permute-start(bf16[2,96,256]{2,1,0:T(8,128)(2,1)S(1)} %fusion.13), channel_id=1, source_target_pairs={{0,256},{256,0},{1,257},{257,1},{2,258},{258,2},{3,259},{259,3},{4... | collective-permute-start | bytes 294920 | tf_op jit(solution)/shard_map/ppermute | solution.py:28
  272.5 8.5 %collective-permute-done.17 = bf16[2,96,256]{2,1,0:T(8,128)(2,1)S(1)} collective-permute-done((bf16[2,96,256]{2,1,0:T(8,128)(2,1)S(1)}, bf16[2,96,256]{2,1,0:T(8,128)(2,1)S(1)}, u32[]{:S(2)}, u32[]{:S(2)}) %collective-permute-start.17) | collective-permute-done | bytes 98336 | tf_op jit(solution)/shard_map/ppermute | solution.py:28
  (84 shorter events, 37.7 us)
Async XLA Ops:
  0.6 6.9 %copy-start.5 = (bf16[256,96]{0,1:T(8,128)(2,1)S(1)}, bf16[256,96]{0,1:T(8,128)(2,1)}, u32[]{:S(2)}) copy-start(bf16[256,96]{0,1:T(8,128)(2,1)} %param.4) | copy-start | bytes 147460
  0.6 7.0 %copy-start.6 = (bf16[256,96]{0,1:T(8,128)(2,1)S(1)}, bf16[256,96]{0,1:T(8,128)(2,1)}, u32[]{:S(2)}) copy-start(bf16[256,96]{0,1:T(8,128)(2,1)} %param.7) | copy-start | bytes 147460
  2.3 29.9 %collective-permute-start = (bf16[2,96,1536]{2,1,0:T(8,128)(2,1)S(1)}, bf16[2,96,1536]{2,1,0:T(8,128)(2,1)S(1)}, u32[]{:S(2)}, u32[]{:S(2)}) collective-permute-start(bf16[2,96,1536]{2,1,0:T(8,128)(2,1)S(1)} %get-tuple-element.29), channel_id=1, source_target_pairs={{0,2},{2,0},{1,3},{3,1},{4,6},{6,4},{5,7},{7,5},{8,10},{10,8},{9,1... | collective-permute-start | bytes 1769480 | tf_op jit(solution)/shard_map/ppermute | solution.py:28
  32.4 29.8 %collective-permute-start.3 = (bf16[2,2,96,1536]{3,2,0,1:T(8,128)(2,1)S(1)}, bf16[2,2,96,1536]{3,2,0,1:T(8,128)(2,1)S(1)}, u32[]{:S(2)}, u32[]{:S(2)}) collective-permute-start(bf16[2,2,96,1536]{3,2,0,1:T(8,128)(2,1)S(1)} %pad_maximum_fusion.3), channel_id=1, source_target_pairs={{0,48},{16,32},{32,16},{48,0},{1,49},{17,33},{33,17},{49,1},{2,50}... | collective-permute-start | bytes 3538952 | tf_op jit(solution)/shard_map/ppermute | solution.py:43
  35.8 29.6 %collective-permute-start.2 = (bf16[2,2,96,1536]{3,2,0,1:T(8,128)(2,1)S(1)}, bf16[2,2,96,1536]{3,2,0,1:T(8,128)(2,1)S(1)}, u32[]{:S(2)}, u32[]{:S(2)}) collective-permute-start(bf16[2,2,96,1536]{3,2,0,1:T(8,128)(2,1)S(1)} %pad_maximum_fusion.3), channel_id=1, source_target_pairs={{0,16},{16,0},{32,48},{48,32},{1,17},{17,1},{33,49},{49,33},{2,18}... | collective-permute-start | bytes 3538952 | tf_op jit(solution)/shard_map/ppermute | solution.py:43
  39.5 18.4 %collective-permute-start.1 = (bf16[192,256]{0,1:T(8,128)(2,1)}, bf16[192,256]{0,1:T(8,128)(2,1)}, u32[]{:S(2)}, u32[]{:S(2)}) collective-permute-start(bf16[192,256]{0,1:T(8,128)(2,1)} %bitcast.3), channel_id=1, source_target_pairs={{0,256},{256,0},{1,257},{257,1},{2,258},{258,2},{3,259},{259,3},{4... | collective-permute-start | bytes 294920 | tf_op jit(solution)/shard_map/ppermute | solution.py:28
  66.5 19.7 %collective-permute-start.4 = (bf16[2,2,96,1536]{3,2,0,1:T(8,128)(2,1)}, bf16[2,2,96,1536]{3,2,0,1:T(8,128)(2,1)}, u32[]{:S(2)}, u32[]{:S(2)}) collective-permute-start(bf16[2,2,96,1536]{3,2,0,1:T(8,128)(2,1)} %broadcast_select_fusion), channel_id=1, source_target_pairs={{0,48},{8,24},{16,32},{24,8},{32,16},{40,56},{48,0},{56,40},{1,49}... | collective-permute-start | bytes 3538952 | tf_op jit(solution)/shard_map/ppermute | solution.py:49
  70.0 10.3 %collective-permute-start.5 = (bf16[384,256]{0,1:T(8,128)(2,1)S(1)}, bf16[384,256]{0,1:T(8,128)(2,1)S(1)}, u32[]{:S(2)}, u32[]{:S(2)}) collective-permute-start(bf16[384,256]{0,1:T(8,128)(2,1)S(1)} %pad_maximum_fusion.14), channel_id=1, source_target_pairs={{0,2},{2,0},{1,3},{3,1},{4,6},{6,4},{5,7},{7,5},{8,10},{10,8},{9,1... | collective-permute-start | bytes 589832 | tf_op jit(solution)/shard_map/ppermute | solution.py:28
  81.8 24.8 %all-to-all-start = ((bf16[4,768,256]{2,1,0:T(8,128)(2,1)}), bf16[4,768,256]{2,1,0:T(8,128)(2,1)}, u32[]{:S(2)}, u32[]{:S(2)}) async-start(bf16[4,768,256]{2,1,0:T(8,128)(2,1)} %broadcast_in_dim.2), calls=%async_computation | async-start | bytes 3145728 | tf_op jit(solution)/shard_map/all_to_all | solution.py:64
  86.2 2.3 copy-start.2
  86.2 2.3 copy-start.3
  86.2 2.3 copy-start.4
  88.5 2.3 copy-start
  88.5 2.3 copy-start.1
  88.7 22.5 %collective-permute-start.6 = (bf16[768,1536]{1,0:T(8,128)(2,1)S(1)}, bf16[768,1536]{1,0:T(8,128)(2,1)}, u32[]{:S(2)}, u32[]{:S(2)}) collective-permute-start(bf16[768,1536]{1,0:T(8,128)(2,1)S(1)} %pad_maximum_fusion.1), channel_id=1, source_target_pairs={{0,8},{8,0},{1,9},{9,1},{2,10},{10,2},{3,11},{11,3},{4,12},{12,4},... | collective-permute-start | bytes 7077896 | tf_op jit(solution)/shard_map/ppermute | solution.py:28
  93.7 24.4 %collective-permute-start.11 = (bf16[768,1536]{1,0:T(8,128)(2,1)}, bf16[768,1536]{1,0:T(8,128)(2,1)}, u32[]{:S(2)}, u32[]{:S(2)}) collective-permute-start(bf16[768,1536]{1,0:T(8,128)(2,1)} %pad_maximum_fusion), channel_id=1, source_target_pairs={{0,8},{8,0},{1,9},{9,1},{2,10},{10,2},{3,11},{11,3},{4,12},{12,4},... | collective-permute-start | bytes 7077896 | tf_op jit(solution)/shard_map/ppermute | solution.py:28
  113.7 12.5 %collective-permute-start.7 = (bf16[128,1536]{1,0:T(8,128)(2,1)S(1)}, bf16[128,1536]{1,0:T(8,128)(2,1)S(1)}, u32[]{:S(2)}, u32[]{:S(2)}) collective-permute-start(bf16[128,1536]{1,0:T(8,128)(2,1)S(1)} %slice.145), channel_id=1, source_target_pairs={{0,1},{1,0},{2,3},{3,2},{4,5},{5,4},{6,7},{7,6},{8,9},{9,8},{10,11... | collective-permute-start | bytes 1179656 | tf_op jit(solution)/shard_map/ppermute | solution.py:28
  120.6 14.8 %collective-permute-start.12 = (bf16[128,1536]{1,0:T(8,128)(2,1)S(1)}, bf16[128,1536]{1,0:T(8,128)(2,1)S(1)}, u32[]{:S(2)}, u32[]{:S(2)}) collective-permute-start(bf16[128,1536]{1,0:T(8,128)(2,1)S(1)} %slice.151), channel_id=1, source_target_pairs={{0,1},{1,0},{2,3},{3,2},{4,5},{5,4},{6,7},{7,6},{8,9},{9,8},{10,11... | collective-permute-start | bytes 1179656 | tf_op jit(solution)/shard_map/ppermute | solution.py:28
  126.3 35.5 %collective-permute-start.8 = (bf16[64,1536]{1,0:T(8,128)(2,1)S(1)}, bf16[64,1536]{1,0:T(8,128)(2,1)S(1)}, u32[]{:S(2)}, u32[]{:S(2)}) collective-permute-start(bf16[64,1536]{1,0:T(8,128)(2,1)S(1)} %slice.147), channel_id=1, source_target_pairs={{0,4},{4,0},{1,5},{5,1},{2,6},{6,2},{3,7},{7,3},{8,12},{12,8},{9,1... | collective-permute-start | bytes 589832 | tf_op jit(solution)/shard_map/ppermute | solution.py:28
  135.6 31.6 %collective-permute-start.13 = (bf16[64,1536]{1,0:T(8,128)(2,1)S(1)}, bf16[64,1536]{1,0:T(8,128)(2,1)S(1)}, u32[]{:S(2)}, u32[]{:S(2)}) collective-permute-start(bf16[64,1536]{1,0:T(8,128)(2,1)S(1)} %slice.153), channel_id=1, source_target_pairs={{0,4},{4,0},{1,5},{5,1},{2,6},{6,2},{3,7},{7,3},{8,12},{12,8},{9,1... | collective-permute-start | bytes 589832 | tf_op jit(solution)/shard_map/ppermute | solution.py:28
  167.5 12.1 %collective-permute-start.9 = (bf16[64,1536]{1,0:T(8,128)(2,1)S(1)}, bf16[64,1536]{1,0:T(8,128)(2,1)S(1)}, u32[]{:S(2)}, u32[]{:S(2)}) collective-permute-start(bf16[64,1536]{1,0:T(8,128)(2,1)S(1)} %get-tuple-element.30), channel_id=1, source_target_pairs={{0,4},{4,0},{1,5},{5,1},{2,6},{6,2},{3,7},{7,3},{8,12},{12,8},{9,1... | collective-permute-start | bytes 589832 | tf_op jit(solution)/shard_map/ppermute | solution.py:28
  176.0 22.3 %collective-permute-start.14 = (bf16[64,1536]{1,0:T(8,128)(2,1)S(1)}, bf16[64,1536]{1,0:T(8,128)(2,1)S(1)}, u32[]{:S(2)}, u32[]{:S(2)}) collective-permute-start(bf16[64,1536]{1,0:T(8,128)(2,1)S(1)} %get-tuple-element.31), channel_id=1, source_target_pairs={{0,4},{4,0},{1,5},{5,1},{2,6},{6,2},{3,7},{7,3},{8,12},{12,8},{9,1... | collective-permute-start | bytes 589832 | tf_op jit(solution)/shard_map/ppermute | solution.py:28
  179.6 24.5 %collective-permute-start.10 = (bf16[128,1536]{1,0:T(8,128)(2,1)S(1)}, bf16[128,1536]{1,0:T(8,128)(2,1)S(1)}, u32[]{:S(2)}, u32[]{:S(2)}) collective-permute-start(bf16[128,1536]{1,0:T(8,128)(2,1)S(1)} %pad_maximum_fusion.8), channel_id=1, source_target_pairs={{0,1},{1,0},{2,3},{3,2},{4,5},{5,4},{6,7},{7,6},{8,9},{9,8},{10,11... | collective-permute-start | bytes 1179656 | tf_op jit(solution)/shard_map/ppermute | solution.py:28
  198.3 11.3 %collective-permute-start.15 = (bf16[128,1536]{1,0:T(8,128)(2,1)S(1)}, bf16[128,1536]{1,0:T(8,128)(2,1)S(1)}, u32[]{:S(2)}, u32[]{:S(2)}) collective-permute-start(bf16[128,1536]{1,0:T(8,128)(2,1)S(1)} %pad_maximum_fusion.9), channel_id=1, source_target_pairs={{0,1},{1,0},{2,3},{3,2},{4,5},{5,4},{6,7},{7,6},{8,9},{9,8},{10,11... | collective-permute-start | bytes 1179656 | tf_op jit(solution)/shard_map/ppermute | solution.py:28
  232.7 26.2 %collective-permute-start.16 = (bf16[2,2,96,256]{3,2,1,0:T(8,128)(2,1)S(1)}, bf16[2,2,96,256]{3,2,1,0:T(8,128)(2,1)S(1)}, u32[]{:S(2)}, u32[]{:S(2)}) collective-permute-start(bf16[2,2,96,256]{3,2,1,0:T(8,128)(2,1)S(1)} %bitcast.111), channel_id=1, source_target_pairs={{0,2},{2,0},{1,3},{3,1},{4,6},{6,4},{5,7},{7,5},{8,10},{10,8},{9,1... | collective-permute-start | bytes 589832 | tf_op jit(solution)/shard_map/ppermute | solution.py:28
  259.0 22.0 %collective-permute-start.17 = (bf16[2,96,256]{2,1,0:T(8,128)(2,1)S(1)}, bf16[2,96,256]{2,1,0:T(8,128)(2,1)S(1)}, u32[]{:S(2)}, u32[]{:S(2)}) collective-permute-start(bf16[2,96,256]{2,1,0:T(8,128)(2,1)S(1)} %fusion.13), channel_id=1, source_target_pairs={{0,256},{256,0},{1,257},{257,1},{2,258},{258,2},{3,259},{259,3},{4... | collective-permute-start | bytes 294920 | tf_op jit(solution)/shard_map/ppermute | solution.py:28

commit v5 on v4

--- a/solution.py
+++ b/solution.py
@@ -58,8 +58,7 @@
     return blocks.reshape(columns.shape)
 
 
-def gathered_rows(both):
-    quad = jnp.concatenate([both, swap(both, "z2")], 0)
+def gathered_rows(quad):
     sent = jnp.broadcast_to(quad[None], (4, 768, 256)).reshape(3072, 256)
     rows = lax.all_to_all(sent, "y", 0, 0, tiled=True)
     rows = rows.reshape(4, 2, 2, 2, 96, 256).transpose(3, 2, 0, 1, 4, 5)
@@ -115,11 +114,11 @@
 def local(tokens, up_weight, down_weight, grad_output):
     shards = own_order(jnp.concatenate([tokens.T, grad_output.T], 0))
     halves = half_swapped(jnp.stack([up_weight, down_weight.T]))
-    shards, halves = lax.optimization_barrier((shards, halves))
     both = jnp.concatenate([shards, swap(shards, "zh")], 0)
+    quad = jnp.concatenate([both, swap(both, "z2")], 0)
     one, three = neighbours(halves)
-    both, one, three = lax.optimization_barrier((both, one, three))
-    rows = gathered_rows(both)
+    quad, one, three = lax.optimization_barrier((quad, one, three))
+    rows = gathered_rows(quad)
     up_own, down_own = over_x(halves, one, three)
     up_other, down_other = swap(up_own, "core"), swap(down_own, "core")
     rows = core_x_order(rows.reshape(2, 2, 2, 2, 192, 256).transpose(1, 2, 3, 0, 4, 5))

time: 284 us -> 294 us (1.035)
  the two profiles are of different devices: /device:TPU:34 before, /device:TPU:24 now
where the time goes in v5:
time: 294 us; the launch traced here: 290 us
  starting transfers between devices  113 us (38%)
  waiting for transfers between devices  107 us (36%)
  blocking collectives  22.4 us (8%)
  other arithmetic  19.4 us (7%)
  matrix products  16.4 us (6%)
  local copies, waits for them, and re-layouts  11.4 us (4%)
    ppermute x15, waiting for transfers between devices, swap(): return lax.ppermute(array, axis, SWAP)  99.3 us
    ppermute x15, starting transfers between devices, swap(): return lax.ppermute(array, axis, SWAP)  97.7 us
    all_to_all x1, blocking collectives, over_gx(): parts = lax.all_to_all(sent, 'y', 0, 0, tiled=True)  22.4 us
    dot_general x8, matrix products, contract(): lax.dot_general(left, right, (dims, ((), ())), preferred_element_type=jnp...  16.4 us
    ppermute x2, starting transfers between devices, neighbours(): lax.ppermute(block, 'x', [(i, i ^ k) for i in range(4)])  7.39 us
    ppermute x1, waiting for transfers between devices, over_x(): two = lax.ppermute(carried, ('x', 'core'), onward)  7.33 us
  transfers between devices with their start and end apart: 19, of which 12 were waited for; matrix products, arithmetic and copies ran while one was open for 12% of the time, Pallas kernels for 0%

profile of v5, /device:TPU:24, one launch (start us, length us, event | category | flops | bytes accessed | tf_op | source)
XLA Modules:
  0.0 290.1 jit_solution(7884676009106134436)
XLA Ops:
  2.3 5.2 %collective-permute-start = (bf16[2,96,1536]{2,1,0:T(8,128)(2,1)S(1)}, bf16[2,96,1536]{2,1,0:T(8,128)(2,1)S(1)}, u32[]{:S(2)}, u32[]{:S(2)}) collective-permute-start(bf16[2,96,1536]{2,1,0:T(8,128)(2,1)S(1)} %get-tuple-element.25), channel_id=1, source_target_pairs={{0,2},{2,0},{1,3},{3,1},{4,6},{6,4},{5,7},{7,5},{8,10},{10,8},{9,1... | collective-permute-start | bytes 1769480 | tf_op jit(solution)/shard_map/ppermute | solution.py:28
  7.5 26.0 %collective-permute-done = bf16[2,96,1536]{2,1,0:T(8,128)(2,1)S(1)} collective-permute-done((bf16[2,96,1536]{2,1,0:T(8,128)(2,1)S(1)}, bf16[2,96,1536]{2,1,0:T(8,128)(2,1)S(1)}, u32[]{:S(2)}, u32[]{:S(2)}) %collective-permute-start) | collective-permute-done | bytes 589856 | tf_op jit(solution)/shard_map/ppermute | solution.py:28
  34.6 3.4 %collective-permute-start.3 = (bf16[2,2,96,1536]{3,2,0,1:T(8,128)(2,1)}, bf16[2,2,96,1536]{3,2,0,1:T(8,128)(2,1)S(1)}, u32[]{:S(2)}, u32[]{:S(2)}) collective-permute-start(bf16[2,2,96,1536]{3,2,0,1:T(8,128)(2,1)} %pad_maximum_fusion.3), channel_id=1, source_target_pairs={{0,16},{16,0},{32,48},{48,32},{1,17},{17,1},{33,49},{49,33},{2,18}... | collective-permute-start | bytes 3538952 | tf_op jit(solution)/shard_map/ppermute | solution.py:43
  38.0 4.0 %collective-permute-start.4 = (bf16[2,2,96,1536]{3,2,0,1:T(8,128)(2,1)}, bf16[2,2,96,1536]{3,2,0,1:T(8,128)(2,1)S(1)}, u32[]{:S(2)}, u32[]{:S(2)}) collective-permute-start(bf16[2,2,96,1536]{3,2,0,1:T(8,128)(2,1)} %pad_maximum_fusion.3), channel_id=1, source_target_pairs={{0,48},{16,32},{32,16},{48,0},{1,49},{17,33},{33,17},{49,1},{2,50}... | collective-permute-start | bytes 3538952 | tf_op jit(solution)/shard_map/ppermute | solution.py:43
  46.7 15.1 %collective-permute-start.1 = (bf16[192,256]{0,1:T(8,128)(2,1)}, bf16[192,256]{0,1:T(8,128)(2,1)S(1)}, u32[]{:S(2)}, u32[]{:S(2)}) collective-permute-start(bf16[192,256]{0,1:T(8,128)(2,1)} %bitcast.9), channel_id=1, source_target_pairs={{0,256},{256,0},{1,257},{257,1},{2,258},{258,2},{3,259},{259,3},{4... | collective-permute-start | bytes 294920 | tf_op jit(solution)/shard_map/ppermute | solution.py:28
  61.8 5.8 %collective-permute-done.1 = bf16[192,256]{0,1:T(8,128)(2,1)S(1)} collective-permute-done((bf16[192,256]{0,1:T(8,128)(2,1)}, bf16[192,256]{0,1:T(8,128)(2,1)S(1)}, u32[]{:S(2)}, u32[]{:S(2)}) %collective-permute-start.1) | collective-permute-done | bytes 98336 | tf_op jit(solution)/shard_map/ppermute | solution.py:28
  71.8 9.1 %collective-permute-done.2 = bf16[384,256]{0,1:T(8,128)(2,1)} collective-permute-done((bf16[384,256]{0,1:T(8,128)(2,1)}, bf16[384,256]{0,1:T(8,128)(2,1)}, u32[]{:S(2)}, u32[]{:S(2)}) %collective-permute-start.2) | collective-permute-done | bytes 196640 | tf_op jit(solution)/shard_map/ppermute | solution.py:28
  84.0 3.0 %collective-permute-start.5 = (bf16[2,2,96,1536]{3,2,0,1:T(8,128)(2,1)}, bf16[2,2,96,1536]{3,2,0,1:T(8,128)(2,1)}, u32[]{:S(2)}, u32[]{:S(2)}) collective-permute-start(bf16[2,2,96,1536]{3,2,0,1:T(8,128)(2,1)} %broadcast_select_fusion), channel_id=1, source_target_pairs={{0,48},{8,24},{16,32},{24,8},{32,16},{40,56},{48,0},{56,40},{1,49}... | collective-permute-start | bytes 3538952 | tf_op jit(solution)/shard_map/ppermute | solution.py:49
  90.6 4.7 %all-to-all-start = ((bf16[4,768,256]{2,1,0:T(8,128)(2,1)}), bf16[4,768,256]{2,1,0:T(8,128)(2,1)}, u32[]{:S(2)}, u32[]{:S(2)}) async-start(bf16[4,768,256]{2,1,0:T(8,128)(2,1)} %broadcast_in_dim.2), calls=%async_computation | async-start | bytes 3145728 | tf_op jit(solution)/shard_map/all_to_all | solution.py:63
  96.3 7.3 %collective-permute-done.5 = bf16[2,2,96,1536]{3,2,0,1:T(8,128)(2,1)} collective-permute-done((bf16[2,2,96,1536]{3,2,0,1:T(8,128)(2,1)}, bf16[2,2,96,1536]{3,2,0,1:T(8,128)(2,1)}, u32[]{:S(2)}, u32[]{:S(2)}) %collective-permute-start.5) | collective-permute-done | bytes 1179680 | tf_op jit(solution)/shard_map/ppermute | solution.py:49
  108.0 2.8 pad_maximum_fusion
  110.9 2.4 collective-permute-start.11
  113.3 2.5 reverse_select_fusion.4
  117.9 2.5 fusion
  122.5 2.5 fusion.26
  125.0 2.5 fusion.1
  127.5 3.8 %collective-permute-start.12 = (bf16[128,1536]{1,0:T(8,128)(2,1)S(1)}, bf16[128,1536]{1,0:T(8,128)(2,1)S(1)}, u32[]{:S(2)}, u32[]{:S(2)}) collective-permute-start(bf16[128,1536]{1,0:T(8,128)(2,1)S(1)} %slice.155), channel_id=1, source_target_pairs={{0,1},{1,0},{2,3},{3,2},{4,5},{5,4},{6,7},{7,6},{8,9},{9,8},{10,11... | collective-permute-start | bytes 1179656 | tf_op jit(solution)/shard_map/ppermute | solution.py:28
  131.2 3.0 %collective-permute-done.7 = bf16[128,1536]{1,0:T(8,128)(2,1)S(1)} collective-permute-done((bf16[128,1536]{1,0:T(8,128)(2,1)S(1)}, bf16[128,1536]{1,0:T(8,128)(2,1)S(1)}, u32[]{:S(2)}, u32[]{:S(2)}) %collective-permute-start.7) | collective-permute-done | bytes 393248 | tf_op jit(solution)/shard_map/ppermute | solution.py:28
  134.4 10.7 %collective-permute-start.8 = (bf16[64,1536]{1,0:T(8,128)(2,1)S(1)}, bf16[64,1536]{1,0:T(8,128)(2,1)S(1)}, u32[]{:S(2)}, u32[]{:S(2)}) collective-permute-start(bf16[64,1536]{1,0:T(8,128)(2,1)S(1)} %slice.151), channel_id=1, source_target_pairs={{0,4},{4,0},{1,5},{5,1},{2,6},{6,2},{3,7},{7,3},{8,12},{12,8},{9,1... | collective-permute-start | bytes 589832 | tf_op jit(solution)/shard_map/ppermute | solution.py:28
  145.2 25.1 %collective-permute-start.13 = (bf16[64,1536]{1,0:T(8,128)(2,1)S(1)}, bf16[64,1536]{1,0:T(8,128)(2,1)S(1)}, u32[]{:S(2)}, u32[]{:S(2)}) collective-permute-start(bf16[64,1536]{1,0:T(8,128)(2,1)S(1)} %slice.157), channel_id=1, source_target_pairs={{0,4},{4,0},{1,5},{5,1},{2,6},{6,2},{3,7},{7,3},{8,12},{12,8},{9,1... | collective-permute-start | bytes 589832 | tf_op jit(solution)/shard_map/ppermute | solution.py:28
  170.4 17.5 %collective-permute-done.13 = bf16[64,1536]{1,0:T(8,128)(2,1)S(1)} collective-permute-done((bf16[64,1536]{1,0:T(8,128)(2,1)S(1)}, bf16[64,1536]{1,0:T(8,128)(2,1)S(1)}, u32[]{:S(2)}, u32[]{:S(2)}) %collective-permute-start.13) | collective-permute-done | bytes 196640 | tf_op jit(solution)/shard_map/ppermute | solution.py:28
  190.2 7.8 %collective-permute-start.14 = (bf16[64,1536]{1,0:T(8,128)(2,1)S(1)}, bf16[64,1536]{1,0:T(8,128)(2,1)S(1)}, u32[]{:S(2)}, u32[]{:S(2)}) collective-permute-start(bf16[64,1536]{1,0:T(8,128)(2,1)S(1)} %get-tuple-element.27), channel_id=1, source_target_pairs={{0,4},{4,0},{1,5},{5,1},{2,6},{6,2},{3,7},{7,3},{8,12},{12,8},{9,1... | collective-permute-start | bytes 589832 | tf_op jit(solution)/shard_map/ppermute | solution.py:28
  198.0 14.8 %collective-permute-done.9 = bf16[64,1536]{1,0:T(8,128)(2,1)S(1)} collective-permute-done((bf16[64,1536]{1,0:T(8,128)(2,1)S(1)}, bf16[64,1536]{1,0:T(8,128)(2,1)S(1)}, u32[]{:S(2)}, u32[]{:S(2)}) %collective-permute-start.9) | collective-permute-done | bytes 196640 | tf_op jit(solution)/shard_map/ppermute | solution.py:28
  219.0 7.7 %collective-permute-done.10 = bf16[128,1536]{1,0:T(8,128)(2,1)S(1)} collective-permute-done((bf16[128,1536]{1,0:T(8,128)(2,1)S(1)}, bf16[128,1536]{1,0:T(8,128)(2,1)S(1)}, u32[]{:S(2)}, u32[]{:S(2)}) %collective-permute-start.10) | collective-permute-done | bytes 393248 | tf_op jit(solution)/shard_map/ppermute | solution.py:28
  226.7 2.5 convolution_convert_fusion.2
  229.2 2.5 convolution_convert_fusion.3
  234.1 2.5 convolution_convert_fusion
  238.6 22.4 %all_to_all.15 = bf16[4,768,256]{2,1,0:T(8,128)(2,1)S(1)} all-to-all(bf16[4,768,256]{2,1,0:T(8,128)(2,1)S(1)} %bitcast.81), channel_id=1, replica_groups=mesh['zh'=2,'y'=4,'x'=4,'core'=2,'z4'=2,'z2'=2,'z1'=2] {'y'}, dimensions={0} | all-to-all | bytes 3145728 | tf_op jit(solution)/shard_map/all_to_all | solution.py:93
  261.3 3.1 %collective-permute-start.16 = (bf16[2,2,96,256]{3,2,1,0:T(8,128)(2,1)S(1)}, bf16[2,2,96,256]{3,2,1,0:T(8,128)(2,1)S(1)}, u32[]{:S(2)}, u32[]{:S(2)}) collective-permute-start(bf16[2,2,96,256]{3,2,1,0:T(8,128)(2,1)S(1)} %bitcast.112), channel_id=1, source_target_pairs={{0,2},{2,0},{1,3},{3,1},{4,6},{6,4},{5,7},{7,5},{8,10},{10,8},{9,1... | collective-permute-start | bytes 589832 | tf_op jit(solution)/shard_map/ppermute | solution.py:28
  264.4 8.5 %collective-permute-done.16 = bf16[2,2,96,256]{3,2,1,0:T(8,128)(2,1)S(1)} collective-permute-done((bf16[2,2,96,256]{3,2,1,0:T(8,128)(2,1)S(1)}, bf16[2,2,96,256]{3,2,1,0:T(8,128)(2,1)S(1)}, u32[]{:S(2)}, u32[]{:S(2)}) %collective-permute-start.16) | collective-permute-done | bytes 196640 | tf_op jit(solution)/shard_map/ppermute | solution.py:28
  273.0 12.7 %collective-permute-start.17 = (bf16[2,96,256]{2,1,0:T(8,128)(2,1)S(1)}, bf16[2,96,256]{2,1,0:T(8,128)(2,1)S(1)}, u32[]{:S(2)}, u32[]{:S(2)}) collective-permute-start(bf16[2,96,256]{2,1,0:T(8,128)(2,1)S(1)} %fusion.15), channel_id=1, source_target_pairs={{0,256},{256,0},{1,257},{257,1},{2,258},{258,2},{3,259},{259,3},{4... | collective-permute-start | bytes 294920 | tf_op jit(solution)/shard_map/ppermute | solution.py:28
  285.7 2.7 collective-permute-done.17
  (76 shorter events, 43.0 us)
Async XLA Ops:
  2.3 31.1 %collective-permute-start = (bf16[2,96,1536]{2,1,0:T(8,128)(2,1)S(1)}, bf16[2,96,1536]{2,1,0:T(8,128)(2,1)S(1)}, u32[]{:S(2)}, u32[]{:S(2)}) collective-permute-start(bf16[2,96,1536]{2,1,0:T(8,128)(2,1)S(1)} %get-tuple-element.25), channel_id=1, source_target_pairs={{0,2},{2,0},{1,3},{3,1},{4,6},{6,4},{5,7},{7,5},{8,10},{10,8},{9,1... | collective-permute-start | bytes 1769480 | tf_op jit(solution)/shard_map/ppermute | solution.py:28
  34.6 48.3 %collective-permute-start.3 = (bf16[2,2,96,1536]{3,2,0,1:T(8,128)(2,1)}, bf16[2,2,96,1536]{3,2,0,1:T(8,128)(2,1)S(1)}, u32[]{:S(2)}, u32[]{:S(2)}) collective-permute-start(bf16[2,2,96,1536]{3,2,0,1:T(8,128)(2,1)} %pad_maximum_fusion.3), channel_id=1, source_target_pairs={{0,16},{16,0},{32,48},{48,32},{1,17},{17,1},{33,49},{49,33},{2,18}... | collective-permute-start | bytes 3538952 | tf_op jit(solution)/shard_map/ppermute | solution.py:43
  38.0 44.9 %collective-permute-start.4 = (bf16[2,2,96,1536]{3,2,0,1:T(8,128)(2,1)}, bf16[2,2,96,1536]{3,2,0,1:T(8,128)(2,1)S(1)}, u32[]{:S(2)}, u32[]{:S(2)}) collective-permute-start(bf16[2,2,96,1536]{3,2,0,1:T(8,128)(2,1)} %pad_maximum_fusion.3), channel_id=1, source_target_pairs={{0,48},{16,32},{32,16},{48,0},{1,49},{17,33},{33,17},{49,1},{2,50}... | collective-permute-start | bytes 3538952 | tf_op jit(solution)/shard_map/ppermute | solution.py:43
  46.7 20.8 %collective-permute-start.1 = (bf16[192,256]{0,1:T(8,128)(2,1)}, bf16[192,256]{0,1:T(8,128)(2,1)S(1)}, u32[]{:S(2)}, u32[]{:S(2)}) collective-permute-start(bf16[192,256]{0,1:T(8,128)(2,1)} %bitcast.9), channel_id=1, source_target_pairs={{0,256},{256,0},{1,257},{257,1},{2,258},{258,2},{3,259},{259,3},{4... | collective-permute-start | bytes 294920 | tf_op jit(solution)/shard_map/ppermute | solution.py:28
  67.6 0.6 copy-start.2
  69.9 11.0 %collective-permute-start.2 = (bf16[384,256]{0,1:T(8,128)(2,1)}, bf16[384,256]{0,1:T(8,128)(2,1)}, u32[]{:S(2)}, u32[]{:S(2)}) collective-permute-start(bf16[384,256]{0,1:T(8,128)(2,1)} %pad_maximum_fusion.14), channel_id=1, source_target_pairs={{0,2},{2,0},{1,3},{3,1},{4,6},{6,4},{5,7},{7,5},{8,10},{10,8},{9,1... | collective-permute-start | bytes 589832 | tf_op jit(solution)/shard_map/ppermute | solution.py:28
  84.0 19.6 %collective-permute-start.5 = (bf16[2,2,96,1536]{3,2,0,1:T(8,128)(2,1)}, bf16[2,2,96,1536]{3,2,0,1:T(8,128)(2,1)}, u32[]{:S(2)}, u32[]{:S(2)}) collective-permute-start(bf16[2,2,96,1536]{3,2,0,1:T(8,128)(2,1)} %broadcast_select_fusion), channel_id=1, source_target_pairs={{0,48},{8,24},{16,32},{24,8},{32,16},{40,56},{48,0},{56,40},{1,49}... | collective-permute-start | bytes 3538952 | tf_op jit(solution)/shard_map/ppermute | solution.py:49
  90.6 22.6 %all-to-all-start = ((bf16[4,768,256]{2,1,0:T(8,128)(2,1)}), bf16[4,768,256]{2,1,0:T(8,128)(2,1)}, u32[]{:S(2)}, u32[]{:S(2)}) async-start(bf16[4,768,256]{2,1,0:T(8,128)(2,1)} %broadcast_in_dim.2), calls=%async_computation | async-start | bytes 3145728 | tf_op jit(solution)/shard_map/all_to_all | solution.py:63
  96.3 9.5 %copy-start.1 = (bf16[1,2,96,1536]{3,2,0,1:T(8,128)(2,1)S(1)}, bf16[1,2,96,1536]{3,2,0,1:T(8,128)(2,1)}, u32[]{:S(2)}) copy-start(bf16[1,2,96,1536]{3,2,0,1:T(8,128)(2,1)} %get-tuple-element.17) | copy-start | bytes 1769476
  105.8 2.2 copy-start
  106.0 11.9 %collective-permute-start.6 = (bf16[768,1536]{1,0:T(8,128)(2,1)S(1)}, bf16[768,1536]{1,0:T(8,128)(2,1)}, u32[]{:S(2)}, u32[]{:S(2)}) collective-permute-start(bf16[768,1536]{1,0:T(8,128)(2,1)S(1)} %pad_maximum_fusion.1), channel_id=1, source_target_pairs={{0,8},{8,0},{1,9},{9,1},{2,10},{10,2},{3,11},{11,3},{4,12},{12,4},... | collective-permute-start | bytes 7077896 | tf_op jit(solution)/shard_map/ppermute | solution.py:28
  110.9 14.1 %collective-permute-start.11 = (bf16[768,1536]{1,0:T(8,128)(2,1)}, bf16[768,1536]{1,0:T(8,128)(2,1)}, u32[]{:S(2)}, u32[]{:S(2)}) collective-permute-start(bf16[768,1536]{1,0:T(8,128)(2,1)} %pad_maximum_fusion), channel_id=1, source_target_pairs={{0,8},{8,0},{1,9},{9,1},{2,10},{10,2},{3,11},{11,3},{4,12},{12,4},... | collective-permute-start | bytes 7077896 | tf_op jit(solution)/shard_map/ppermute | solution.py:28
  120.4 13.9 %collective-permute-start.7 = (bf16[128,1536]{1,0:T(8,128)(2,1)S(1)}, bf16[128,1536]{1,0:T(8,128)(2,1)S(1)}, u32[]{:S(2)}, u32[]{:S(2)}) collective-permute-start(bf16[128,1536]{1,0:T(8,128)(2,1)S(1)} %slice.149), channel_id=1, source_target_pairs={{0,1},{1,0},{2,3},{3,2},{4,5},{5,4},{6,7},{7,6},{8,9},{9,8},{10,11... | collective-permute-start | bytes 1179656 | tf_op jit(solution)/shard_map/ppermute | solution.py:28
  127.5 17.6 %collective-permute-start.12 = (bf16[128,1536]{1,0:T(8,128)(2,1)S(1)}, bf16[128,1536]{1,0:T(8,128)(2,1)S(1)}, u32[]{:S(2)}, u32[]{:S(2)}) collective-permute-start(bf16[128,1536]{1,0:T(8,128)(2,1)S(1)} %slice.155), channel_id=1, source_target_pairs={{0,1},{1,0},{2,3},{3,2},{4,5},{5,4},{6,7},{7,6},{8,9},{9,8},{10,11... | collective-permute-start | bytes 1179656 | tf_op jit(solution)/shard_map/ppermute | solution.py:28
  134.4 36.0 %collective-permute-start.8 = (bf16[64,1536]{1,0:T(8,128)(2,1)S(1)}, bf16[64,1536]{1,0:T(8,128)(2,1)S(1)}, u32[]{:S(2)}, u32[]{:S(2)}) collective-permute-start(bf16[64,1536]{1,0:T(8,128)(2,1)S(1)} %slice.151), channel_id=1, source_target_pairs={{0,4},{4,0},{1,5},{5,1},{2,6},{6,2},{3,7},{7,3},{8,12},{12,8},{9,1... | collective-permute-start | bytes 589832 | tf_op jit(solution)/shard_map/ppermute | solution.py:28
  145.2 42.7 %collective-permute-start.13 = (bf16[64,1536]{1,0:T(8,128)(2,1)S(1)}, bf16[64,1536]{1,0:T(8,128)(2,1)S(1)}, u32[]{:S(2)}, u32[]{:S(2)}) collective-permute-start(bf16[64,1536]{1,0:T(8,128)(2,1)S(1)} %slice.157), channel_id=1, source_target_pairs={{0,4},{4,0},{1,5},{5,1},{2,6},{6,2},{3,7},{7,3},{8,12},{12,8},{9,1... | collective-permute-start | bytes 589832 | tf_op jit(solution)/shard_map/ppermute | solution.py:28
  188.3 24.5 %collective-permute-start.9 = (bf16[64,1536]{1,0:T(8,128)(2,1)S(1)}, bf16[64,1536]{1,0:T(8,128)(2,1)S(1)}, u32[]{:S(2)}, u32[]{:S(2)}) collective-permute-start(bf16[64,1536]{1,0:T(8,128)(2,1)S(1)} %get-tuple-element.26), channel_id=1, source_target_pairs={{0,4},{4,0},{1,5},{5,1},{2,6},{6,2},{3,7},{7,3},{8,12},{12,8},{9,1... | collective-permute-start | bytes 589832 | tf_op jit(solution)/shard_map/ppermute | solution.py:28
  190.2 26.8 %collective-permute-start.14 = (bf16[64,1536]{1,0:T(8,128)(2,1)S(1)}, bf16[64,1536]{1,0:T(8,128)(2,1)S(1)}, u32[]{:S(2)}, u32[]{:S(2)}) collective-permute-start(bf16[64,1536]{1,0:T(8,128)(2,1)S(1)} %get-tuple-element.27), channel_id=1, source_target_pairs={{0,4},{4,0},{1,5},{5,1},{2,6},{6,2},{3,7},{7,3},{8,12},{12,8},{9,1... | collective-permute-start | bytes 589832 | tf_op jit(solution)/shard_map/ppermute | solution.py:28
  212.8 13.9 %collective-permute-start.10 = (bf16[128,1536]{1,0:T(8,128)(2,1)S(1)}, bf16[128,1536]{1,0:T(8,128)(2,1)S(1)}, u32[]{:S(2)}, u32[]{:S(2)}) collective-permute-start(bf16[128,1536]{1,0:T(8,128)(2,1)S(1)} %pad_maximum_fusion.8), channel_id=1, source_target_pairs={{0,1},{1,0},{2,3},{3,2},{4,5},{5,4},{6,7},{7,6},{8,9},{9,8},{10,11... | collective-permute-start | bytes 1179656 | tf_op jit(solution)/shard_map/ppermute | solution.py:28
  217.1 17.0 %collective-permute-start.15 = (bf16[128,1536]{1,0:T(8,128)(2,1)S(1)}, bf16[128,1536]{1,0:T(8,128)(2,1)S(1)}, u32[]{:S(2)}, u32[]{:S(2)}) collective-permute-start(bf16[128,1536]{1,0:T(8,128)(2,1)S(1)} %pad_maximum_fusion.9), channel_id=1, source_target_pairs={{0,1},{1,0},{2,3},{3,2},{4,5},{5,4},{6,7},{7,6},{8,9},{9,8},{10,11... | collective-permute-start | bytes 1179656 | tf_op jit(solution)/shard_map/ppermute | solution.py:28
  261.3 11.7 %collective-permute-start.16 = (bf16[2,2,96,256]{3,2,1,0:T(8,128)(2,1)S(1)}, bf16[2,2,96,256]{3,2,1,0:T(8,128)(2,1)S(1)}, u32[]{:S(2)}, u32[]{:S(2)}) collective-permute-start(bf16[2,2,96,256]{3,2,1,0:T(8,128)(2,1)S(1)} %bitcast.112), channel_id=1, source_target_pairs={{0,2},{2,0},{1,3},{3,1},{4,6},{6,4},{5,7},{7,5},{8,10},{10,8},{9,1... | collective-permute-start | bytes 589832 | tf_op jit(solution)/shard_map/ppermute | solution.py:28
  273.0 15.4 %collective-permute-start.17 = (bf16[2,96,256]{2,1,0:T(8,128)(2,1)S(1)}, bf16[2,96,256]{2,1,0:T(8,128)(2,1)S(1)}, u32[]{:S(2)}, u32[]{:S(2)}) collective-permute-start(bf16[2,96,256]{2,1,0:T(8,128)(2,1)S(1)} %fusion.15), channel_id=1, source_target_pairs={{0,256},{256,0},{1,257},{257,1},{2,258},{258,2},{3,259},{259,3},{4... | collective-permute-start | bytes 294920 | tf_op jit(solution)/shard_map/ppermute | solution.py:28
